TPU v7x, 32 devices: a whole 2x2x4 slice. The times are simulated.
32 devices in a mesh: dp: 16 (over z, y, x), tensor: 2 (over core).
Axes of the slice: x: 2, y: 2, z: 4, core: 2. Of those that a mesh axis runs over, the one named last changes fastest.
Arguments:
- tokens: bfloat16 [16384, 1024], P(('dp', 'tensor')), may hold values from -6 to 6
- segments: int32 [16, 1024], P('dp'), may hold values from 0 to 256, as said below
- norm1_gain: float32 [1024], replicated, may hold values from 0.25 to 1.75
- in_weight: bfloat16 [1024, 3, 1024], P(None, None, 'tensor'), may hold values from -0.1875 to 0.1875
- conv_kernel: float32 [3, 1024], P(None, 'tensor'), may hold values from -3.5 to 3.5
- out_weight: bfloat16 [1024, 1024], P('tensor'), may hold values from -0.1875 to 0.1875
- norm2_gain: float32 [1024], replicated, may hold values from 0.25 to 1.75
- gate_weight: bfloat16 [1024, 4608], P(None, 'tensor'), may hold values from -0.1875 to 0.1875
- up_weight: bfloat16 [1024, 4608], P(None, 'tensor'), may hold values from -0.1875 to 0.1875
- down_weight: bfloat16 [4608, 1024], P('tensor'), may hold values from -0.09375 to 0.09375
- cotangent: bfloat16 [16384, 1024], P(('dp', 'tensor')), may hold values from -12 to 12
Outputs:
- mixed: bfloat16 [16384, 1024], P(('dp', 'tensor'))
- input_grad: float32 [16384, 1024], P(('dp', 'tensor'))
- norm1_grad: float32 [1024], P('tensor')
- in_grad: float32 [1024, 3, 1024], P('dp', None, 'tensor')
- kernel_grad: float32 [3, 1024], P(None, 'tensor')
- out_grad: float32 [1024, 1024], P('tensor', 'dp')
- norm2_grad: float32 [1024], P('tensor')
- gate_grad: float32 [1024, 4608], P('dp', 'tensor')
- up_grad: float32 [1024, 4608], P('dp', 'tensor')
- down_grad: float32 [4608, 1024], P('tensor', 'dp')
Inputs may be any that keep to these rules, and one draw needn't show every extreme that they name: `segments`: along each row the numbers start at 0, never fall and rise by at most one from a token to the next; every row ends at the largest value; in each row one document covers every position from below 512 up to 512.
All inputs are finite; a program needn't handle non-finite values.
Results may differ from a plain program's by a relative error of at most 0.018.
Values may be sent and summed in bfloat16 or wider, within the bound.
A program may use at most 192 MiB of HBM per device.

v0:
```python
import jax
import jax.numpy as jnp
from jax import lax
from jax.sharding import PartitionSpec as P

EPSILON = 1e-06


def normalize(values):
    inverse = lax.rsqrt(jnp.mean(values * values, axis=-1, keepdims=True) + EPSILON)
    return (values * inverse, inverse)


def norm_back(grad_norm, unit_rows, inverse, scales):
    grad_unit = grad_norm * scales
    grad_in = inverse * (
        grad_unit - unit_rows * jnp.mean(grad_unit * unit_rows, axis=-1, keepdims=True)
    )
    return (grad_in, jnp.sum(grad_norm * unit_rows, axis=0))


def lagged(values, lag_steps):
    return jnp.concatenate([jnp.zeros_like(values[:lag_steps]), values[:-lag_steps]], axis=0)


def leading(values, lag_steps):
    return jnp.concatenate([values[lag_steps:], jnp.zeros_like(values[:lag_steps])], axis=0)


def doc_mask(seg_row, lag_steps):
    same_doc = jnp.concatenate(
        [
            jnp.zeros((lag_steps,), jnp.int32),
            (seg_row[lag_steps:] == seg_row[:-lag_steps]).astype(jnp.int32),
        ]
    )
    return same_doc[:, None].astype(jnp.float32)


def dot_nt(left, right):
    return lax.dot_general(
        left, right, (((1,), (1,)), ((), ())), preferred_element_type=jnp.float32
    )


def dot_tn(left, right):
    return lax.dot_general(
        left, right, (((0,), (0,)), ((), ())), preferred_element_type=jnp.float32
    )


def local(
    tokens,
    segments,
    norm1_gain,
    in_weight,
    conv_kernel,
    out_weight,
    norm2_gain,
    gate_weight,
    up_weight,
    down_weight,
    cotangent,
):
    local_ch = conv_kernel.shape[1]
    taps = conv_kernel.shape[0]
    seg_row = segments[0]
    inputs = tokens.astype(jnp.float32)
    unit1, inv1 = normalize(inputs)
    norm1 = (unit1 * norm1_gain).astype(jnp.bfloat16)
    norm1_all = lax.all_gather(norm1, "tensor", axis=0, tiled=True)
    projected = jnp.einsum("td,dkc->tkc", norm1_all, in_weight, preferred_element_type=jnp.float32)
    b_gate = projected[:, 0]
    c_gate = projected[:, 1]
    x_gate = projected[:, 2]
    gated = b_gate * x_gate
    conv_out = conv_kernel[taps - 1] * gated
    masks = []
    masked_lags = []
    for tap_index in range(taps - 1):
        lag_steps = taps - 1 - tap_index
        tap_mask = doc_mask(seg_row, lag_steps)
        masked = lagged(gated, lag_steps) * tap_mask
        masks.append(tap_mask)
        masked_lags.append(masked)
        conv_out = conv_out + conv_kernel[tap_index] * masked
    mixer_act = (c_gate * conv_out).astype(jnp.bfloat16)
    mixer_out = lax.psum_scatter(
        jnp.dot(mixer_act, out_weight, preferred_element_type=jnp.float32),
        "tensor",
        scatter_dimension=0,
        tiled=True,
    )
    middle = inputs + mixer_out
    unit2, inv2 = normalize(middle)
    norm2 = (unit2 * norm2_gain).astype(jnp.bfloat16)
    norm2_all = lax.all_gather(norm2, "tensor", axis=0, tiled=True)
    gate_val = jnp.dot(norm2_all, gate_weight, preferred_element_type=jnp.float32)
    up_val = jnp.dot(norm2_all, up_weight, preferred_element_type=jnp.float32)
    sigma = jax.nn.sigmoid(gate_val)
    silu_val = gate_val * sigma
    hidden = (silu_val * up_val).astype(jnp.bfloat16)
    ffn_out = lax.psum_scatter(
        jnp.dot(hidden, down_weight, preferred_element_type=jnp.float32).astype(jnp.bfloat16),
        "tensor",
        scatter_dimension=0,
        tiled=True,
    ).astype(jnp.float32)
    mixed = (middle + ffn_out).astype(jnp.bfloat16)
    cot_rows = cotangent.astype(jnp.float32)
    cot_all = lax.all_gather(cotangent, "tensor", axis=0, tiled=True)
    d_hidden = dot_nt(cot_all, down_weight)
    down_part = dot_tn(hidden, cot_all)
    d_gate = (d_hidden * up_val * sigma * (1.0 + gate_val * (1.0 - sigma))).astype(jnp.bfloat16)
    d_up = (d_hidden * silu_val).astype(jnp.bfloat16)
    gate_part = dot_tn(norm2_all, d_gate)
    up_part = dot_tn(norm2_all, d_up)
    d_norm2 = lax.psum_scatter(
        dot_nt(d_gate, gate_weight) + dot_nt(d_up, up_weight),
        "tensor",
        scatter_dimension=0,
        tiled=True,
    )
    d_mid_norm, gain2_part = norm_back(d_norm2, unit2, inv2, norm2_gain)
    d_middle = cot_rows + d_mid_norm
    d_middle_all = lax.all_gather(d_middle.astype(jnp.bfloat16), "tensor", axis=0, tiled=True)
    d_mixer = dot_nt(d_middle_all, out_weight)
    out_part = dot_tn(mixer_act, d_middle_all)
    d_conv = d_mixer * c_gate
    d_c = d_mixer * conv_out
    d_gated = conv_kernel[taps - 1] * d_conv
    kernel_rows = []
    for tap_index in range(taps - 1):
        lag_steps = taps - 1 - tap_index
        d_gated = d_gated + conv_kernel[tap_index] * leading(d_conv * masks[tap_index], lag_steps)
        kernel_rows.append(jnp.sum(d_conv * masked_lags[tap_index], axis=0))
    kernel_rows.append(jnp.sum(d_conv * gated, axis=0))
    kernel_part = jnp.stack(kernel_rows, axis=0)
    d_projected = jnp.stack([d_gated * x_gate, d_c, d_gated * b_gate], axis=1).astype(jnp.bfloat16)
    in_part = jnp.einsum("td,tkc->dkc", norm1_all, d_projected, preferred_element_type=jnp.float32)
    d_norm1 = lax.psum_scatter(
        jnp.einsum(
            "tkc,dkc->td", d_projected, in_weight, preferred_element_type=jnp.float32
        ).astype(jnp.bfloat16),
        "tensor",
        scatter_dimension=0,
        tiled=True,
    ).astype(jnp.float32)
    d_in_norm, gain1_part = norm_back(d_norm1, unit1, inv1, norm1_gain)
    input_grad = d_middle + d_in_norm
    gain1_total, gain2_total = lax.psum((gain1_part, gain2_part), ("dp", "tensor"))
    kernel_grad = lax.psum(kernel_part, "dp")
    in_total, gate_total, up_total, out_total, down_total = (
        lax.psum_scatter(
            in_part.astype(jnp.bfloat16), "dp", scatter_dimension=0, tiled=True
        ).astype(jnp.float32),
        lax.psum_scatter(
            gate_part.astype(jnp.bfloat16), "dp", scatter_dimension=0, tiled=True
        ).astype(jnp.float32),
        lax.psum_scatter(
            up_part.astype(jnp.bfloat16), "dp", scatter_dimension=0, tiled=True
        ).astype(jnp.float32),
        lax.psum_scatter(
            out_part.astype(jnp.bfloat16), "dp", scatter_dimension=1, tiled=True
        ).astype(jnp.float32),
        lax.psum_scatter(
            down_part.astype(jnp.bfloat16), "dp", scatter_dimension=1, tiled=True
        ).astype(jnp.float32),
    )
    channel_start = lax.axis_index("tensor") * local_ch
    norm1_grad = lax.dynamic_slice_in_dim(gain1_total, channel_start, local_ch, 0)
    norm2_grad = lax.dynamic_slice_in_dim(gain2_total, channel_start, local_ch, 0)
    return (
        mixed,
        input_grad,
        norm1_grad,
        in_total,
        kernel_grad,
        out_total,
        norm2_grad,
        gate_total,
        up_total,
        down_total,
    )


def solution(mesh):
    in_specs = (
        P(("dp", "tensor"), None),
        P("dp", None),
        P(),
        P(None, None, "tensor"),
        P(None, "tensor"),
        P("tensor", None),
        P(),
        P(None, "tensor"),
        P(None, "tensor"),
        P("tensor", None),
        P(("dp", "tensor"), None),
    )
    out_specs = (
        P(("dp", "tensor"), None),
        P(("dp", "tensor"), None),
        P("tensor"),
        P("dp", None, "tensor"),
        P(None, "tensor"),
        P("tensor", "dp"),
        P("tensor"),
        P("dp", "tensor"),
        P("dp", "tensor"),
        P("tensor", "dp"),
    )
    return jax.shard_map(local, mesh=mesh, in_specs=in_specs, out_specs=out_specs, check_vma=False)
```

profile of v0, /device:TPU:0, one launch (start us, length us, event | category | flops | bytes accessed | tf_op | source)
XLA Modules:
  0.0 782.1 jit_solution(1178972347512979289)
XLA Ops:
  7.3 1.7 fusion.11
  8.9 2.5 fusion.8
  11.5 0.0 reduce-scatter.10.cloned.1.call-start
  11.5 0.1 compare_reduce_fusion
  11.6 0.1 compare_reduce_fusion.1
  11.7 0.1 convert_convert_fusion
  11.8 13.1 %all-gather.5.cloned.1.call-done = bf16[1024,1024]{1,0:T(8,128)(2,1)} async-done(((bf16[512,1024]{1,0:T(8,128)(2,1)}), bf16[1024,1024]{1,0:T(8,128)(2,1)}) %all-gather.5.cloned.1.call-update) | async-done | bytes 2097168 | tf_op jit(solution)/shard_map/all_gather | solution.py:71
  24.9 5.0 fusion.13
  29.9 0.5 fusion.16
  30.4 2.1 copy-done.4
  32.5 2.4 multiply_convert_fusion.7
  34.9 1.0 copy-done.7
  35.9 3.2 fusion.25
  39.1 0.0 all-gather.7.cloned.1.call-start
  39.2 13.3 %reduce-scatter.10.cloned.1.call-done = f32[512,1024]{1,0:T(8,128)} async-done(((f32[1024,1024]{1,0:T(8,128)}), f32[512,1024]{1,0:T(8,128)}) %reduce-scatter.10.cloned.1.call-update) | async-done | bytes 2097168 | tf_op jit(solution)/shard_map/reduce_scatter | solution.py:88
  52.5 2.2 multiply_reduce_fusion.5
  54.7 1.3 copy-done.2
  56.0 1.2 multiply_convert_fusion.6
  57.3 0.5 all-gather.9.cloned.1.call-update
  57.8 0.2 reduce-scatter.14.cloned.1.call-start
  58.0 11.2 %all-gather.7.cloned.1.call-done = bf16[1024,1024]{1,0:T(8,128)(2,1)} async-done(((bf16[512,1024]{1,0:T(8,128)(2,1)}), bf16[1024,1024]{1,0:T(8,128)(2,1)}) %all-gather.7.cloned.1.call-update) | async-done | bytes 2097168 | tf_op jit(solution)/shard_map/all_gather | solution.py:97
  69.3 10.2 %fusion.26 = f32[1024,2304]{1,0:T(8,128)} fusion(bf16[1024,1024]{1,0:T(8,128)(2,1)} %all-gather.7.cloned.1.call-done, bf16[1024,2304]{1,0:T(8,128)(2,1)} %param.18), kind=kOutput, calls=%fused_computation.73 | convolution fusion | flops 4831838208 | bytes 16252928 | tf_op jit(solution)/shard_map/dot_general | solution.py:98
  79.5 10.1 %fusion.27 = f32[1024,2304]{1,0:T(8,128)} fusion(bf16[1024,1024]{1,0:T(8,128)(2,1)S(1)} %copy-done.15, bf16[1024,2304]{1,0:T(8,128)(2,1)} %param.19), kind=kOutput, calls=%fused_computation.74 | convolution fusion | flops 4831838208 | bytes 16252928 | tf_op jit(solution)/shard_map/dot_general | solution.py:99
  89.5 17.8 %multiply_convert_fusion = (bf16[1024,2304]{1,0:T(8,128)(2,1)}, bf16[1024,2304]{1,0:T(8,128)(2,1)}, bf16[1024,2304]{1,0:T(8,128)(2,1)}) fusion(f32[1024,2304]{1,0:T(8,128)} %fusion.26, f32[1024,2304]{1,0:T(8,128)} %fusion.27, bf16[1024,1024]{1,0:T(8,128)(2,1)} %all-gather.9.cloned.1.call-done, bf16[2304,1024]{1,0:T(8,128)(2,1)} %param.20), kind=kOutput, calls=%fused_computation | convolution fusion | flops 4867227648 | bytes 39845888 | tf_op jit(solution)/shard_map/dot_general | solution.py:41
  107.4 8.5 %fusion.28 = f32[1024,1024]{1,0:T(8,128)S(1)} fusion(bf16[1024,2304]{1,0:T(8,128)(2,1)} %get-tuple-element.27, bf16[1024,2304]{1,0:T(8,128)(2,1)} %param.18), kind=kOutput, calls=%fused_computation.75 | convolution fusion | flops 4831838208 | bytes 13631488 | tf_op jit(solution)/shard_map/dot_general | solution.py:41
  115.9 9.0 %convolution_add_fusion = f32[1024,1024]{1,0:T(8,128)} fusion(f32[1024,1024]{1,0:T(8,128)S(1)} %fusion.28, bf16[1024,2304]{1,0:T(8,128)(2,1)S(1)} %copy-done.16, bf16[1024,2304]{1,0:T(8,128)(2,1)} %param.19), kind=kOutput, calls=%fused_computation.53 | convolution fusion | flops 4832886784 | bytes 17825792 | tf_op jit(solution)/shard_map/dot_general | solution.py:41
  124.9 0.3 all-gather.11.cloned.1.call-start
  125.1 13.1 %reduce-scatter.14.cloned.1.call-done = f32[512,1024]{1,0:T(8,128)} async-done(((f32[1024,1024]{1,0:T(8,128)}), f32[512,1024]{1,0:T(8,128)}) %reduce-scatter.14.cloned.1.call-update) | async-done | bytes 2097168 | tf_op jit(solution)/shard_map/reduce_scatter | solution.py:118
  138.3 3.0 multiply_reduce_fusion
  141.2 0.5 copy-done.5
  141.7 2.8 fusion.22
  144.6 9.4 %convolution_convert_fusion.2 = bf16[1024,2304]{1,0:T(8,128)(2,1)} fusion(bf16[1024,1024]{1,0:T(8,128)(2,1)} %all-gather.7.cloned.1.call-done, bf16[1024,2304]{1,0:T(8,128)(2,1)} %get-tuple-element.27), kind=kOutput, calls=%fused_computation.7 | convolution fusion | flops 4834197504 | bytes 11534336 | tf_op jit(solution)/shard_map/dot_general | solution.py:47
  154.1 9.7 %convolution_convert_fusion.1 = bf16[1024,2304]{1,0:T(8,128)(2,1)} fusion(bf16[1024,1024]{1,0:T(8,128)(2,1)} %all-gather.7.cloned.1.call-done, bf16[1024,2304]{1,0:T(8,128)(2,1)} %get-tuple-element.26), kind=kOutput, calls=%fused_computation.6 | convolution fusion | flops 4834197504 | bytes 11534336 | tf_op jit(solution)/shard_map/dot_general | solution.py:47
  163.9 9.5 %convolution_convert_fusion = bf16[2304,1024]{0,1:T(8,128)(2,1)} fusion(bf16[1024,2304]{1,0:T(8,128)(2,1)} %get-tuple-element.28, bf16[1024,1024]{1,0:T(8,128)(2,1)} %all-gather.9.cloned.1.call-done), kind=kOutput, calls=%fused_computation.5 | convolution fusion | flops 4834197504 | bytes 11534336 | tf_op jit(solution)/shard_map/dot_general | solution.py:47
  173.5 0.1 slice.71
  173.6 0.1 slice.69
  173.6 4.2 convolution_convert_fusion.5
  177.9 0.3 reduce-scatter.16.cloned.1.call-start
  178.2 7.1 multiply_reduce_fusion.3
  185.3 0.3 slice_multiply_fusion
  185.6 0.3 slice_multiply_fusion.1
  185.9 2.7 fusion.17
  188.6 2.3 fusion.19
  191.0 0.9 copy-done.10
  191.9 4.6 bitcast_convert_fusion
  196.6 9.4 %convolution_convert_fusion.4 = bf16[1024,1024]{1,0:T(8,128)(2,1)} fusion(bf16[1024,2304]{1,0:T(8,128)(2,1)} %get-tuple-element.28, bf16[2304,1024]{1,0:T(8,128)(2,1)} %param.20), kind=kOutput, calls=%fused_computation.54 | convolution fusion | flops 4832886784 | bytes 11534336 | tf_op jit(solution)/shard_map/dot_general | solution.py:104
  206.1 7.7 convolution_convert_fusion.3
  213.8 86.5 %reduce-scatter.22.cloned.1.call-done = bf16[64,2304]{1,0:T(8,128)(2,1)} async-done(((bf16[1024,2304]{1,0:T(8,128)(2,1)}), bf16[64,2304]{1,0:T(8,128)(2,1)}) %reduce-scatter.22.cloned.1.call-update) | async-done | bytes 294928 | tf_op jit(solution)/shard_map/reduce_scatter | solution.py:157
  300.4 1.8 convert_element_type.118
  302.2 140.9 %reduce-scatter.24.cloned.1.call-done = bf16[64,2304]{1,0:T(8,128)(2,1)} async-done(((bf16[1024,2304]{1,0:T(8,128)(2,1)}), bf16[64,2304]{1,0:T(8,128)(2,1)}) %reduce-scatter.24.cloned.1.call-update) | async-done | bytes 294928 | tf_op jit(solution)/shard_map/reduce_scatter | solution.py:160
  443.1 1.8 convert_element_type.120
  444.9 139.9 %reduce-scatter.26.cloned.1.call-done = bf16[2304,64]{0,1:T(8,128)(2,1)} async-done(((bf16[2304,1024]{0,1:T(8,128)(2,1)}), bf16[2304,64]{0,1:T(8,128)(2,1)}) %reduce-scatter.26.cloned.1.call-update) | async-done | bytes 294928 | tf_op jit(solution)/shard_map/reduce_scatter | solution.py:166
  584.8 1.8 convert_element_type.122
  586.6 41.1 %psum.22 = f32[3,512]{1,0:T(4,128)} all-reduce(f32[3,512]{1,0:T(4,128)S(1)} %pad_maximum_fusion.3), channel_id=1, replica_groups=mesh['dp'=16,'tensor'=2] {'dp'}, use_global_device_ids=true, to_apply=%region_14.0 | all-reduce | flops 1536 | bytes 12288 | tf_op jit(solution)/shard_map/psum | solution.py:152
  627.8 36.2 %reduce-scatter.20.cloned.1.call-done = bf16[512,64]{0,1:T(8,128)(2,1)} async-done(((bf16[512,1024]{0,1:T(8,128)(2,1)}), bf16[512,64]{0,1:T(8,128)(2,1)}) %reduce-scatter.20.cloned.1.call-update) | async-done | bytes 65552 | tf_op jit(solution)/shard_map/reduce_scatter | solution.py:163
  663.9 1.5 convert_element_type.116
  665.4 7.5 reduce-scatter.16.cloned.1.call-done
  672.9 2.4 fusion.10
  675.3 41.7 %all-reduce.5 = (f32[1024]{0:T(1024)S(1)}, f32[1024]{0:T(1024)S(1)}) all-reduce(f32[1024]{0:T(1024)S(1)} %get-tuple-element.12, f32[1024]{0:T(1024)S(1)} %get-tuple-element.10), channel_id=1, replica_groups=mesh['dp'=16,'tensor'=2] {'dp','tensor'}, use_global_device_ids=true, to_apply=%region_9.0 | all-reduce | flops 2048 | bytes 16384 | tf_op jit(solution)/shard_map/psum | solution.py:151
  717.0 0.7 dynamic_slice.6
  717.6 0.6 dynamic_slice.7
  718.3 5.2 fusion.7
  723.5 50.0 %reduce-scatter.18.cloned.1.call-done = bf16[64,3,512]{2,0,1:T(8,128)(2,1)} async-done(((bf16[1024,3,512]{2,0,1:T(8,128)(2,1)}), bf16[64,3,512]{2,0,1:T(8,128)(2,1)}) %reduce-scatter.18.cloned.1.call-update) | async-done | bytes 196624 | tf_op jit(solution)/shard_map/reduce_scatter | solution.py:154
  773.4 1.7 convert_element_type.114
  (58 shorter events, 0.6 us)
Async XLA Ops:
  7.2 17.7 %copy-start = (bf16[1024,3,512]{2,0,1:T(8,128)(2,1)S(1)}, bf16[1024,3,512]{2,0,1:T(8,128)(2,1)}, u32[]{:S(2)}) copy-start(bf16[1024,3,512]{2,0,1:T(8,128)(2,1)} %param.14) | copy-start | bytes 9437188
  7.2 4.3 copy-start.12
  7.2 4.6 copy-start.14
  7.2 17.7 %all-gather.5.cloned.1.call-start = ((), (), s32[]{:S(2)}) async-start(), calls=%async_computation.9 | async-start | bytes 3145728 | tf_op jit(solution)/shard_map/all_gather | solution.py:71
  11.5 41.0 %reduce-scatter.10.cloned.1.call-start = ((), (), s32[]{:S(2)}) async-start(), calls=%async_computation.10 | async-start | bytes 6291456 | tf_op jit(solution)/shard_map/reduce_scatter | solution.py:88
  29.9 2.6 copy-start.4
  30.4 4.5 copy-start.1
  32.5 3.4 copy-start.6
  34.9 1.0 copy-start.7
  39.1 16.9 %copy-start.11 = (f32[1024]{0:T(1024)S(1)}, f32[1024]{0:T(1024)}, u32[]{:S(2)}) copy-start(f32[1024]{0:T(1024)} %param.17) | copy-start | bytes 12292
  39.1 30.1 %all-gather.7.cloned.1.call-start = ((), (), s32[]{:S(2)}) async-start(), calls=%async_computation.11 | async-start | bytes 3145728 | tf_op jit(solution)/shard_map/all_gather | solution.py:97
  54.7 1.3 copy-start.2
  57.2 32.3 %all-gather.9.cloned.1.call-start = ((), (), s32[]{:S(2)}) async-start(), calls=%async_computation.13 | async-start | bytes 3145728 | tf_op jit(solution)/shard_map/all_gather | solution.py:111
  57.8 80.4 %reduce-scatter.14.cloned.1.call-start = ((), (), s32[]{:S(2)}) async-start(), calls=%async_computation.14 | async-start | bytes 6291456 | tf_op jit(solution)/shard_map/reduce_scatter | solution.py:118
  69.3 10.2 %copy-start.15 = (bf16[1024,1024]{1,0:T(8,128)(2,1)S(1)}, bf16[1024,1024]{1,0:T(8,128)(2,1)}, u32[]{:S(2)}) copy-start(bf16[1024,1024]{1,0:T(8,128)(2,1)} %all-gather.7.cloned.1.call-done) | copy-start | bytes 6291460
  107.4 8.5 %copy-start.16 = (bf16[1024,2304]{1,0:T(8,128)(2,1)S(1)}, bf16[1024,2304]{1,0:T(8,128)(2,1)}, u32[]{:S(2)}) copy-start(bf16[1024,2304]{1,0:T(8,128)(2,1)} %get-tuple-element.26) | copy-start | bytes 14155780
  124.9 48.8 %all-gather.11.cloned.1.call-start = ((), (), s32[]{:S(2)}) async-start(), calls=%async_computation.15 | async-start | bytes 3145728 | tf_op jit(solution)/shard_map/all_gather | solution.py:126
  138.2 3.0 copy-start.3
  138.3 3.5 copy-start.5
  144.6 155.8 %reduce-scatter.22.cloned.1.call-start = ((), (), s32[]{:S(2)}) async-start(), calls=%async_computation.19 | async-start | bytes 5013504 | tf_op jit(solution)/shard_map/reduce_scatter | solution.py:157
  154.0 289.1 %reduce-scatter.24.cloned.1.call-start = ((), (), s32[]{:S(2)}) async-start(), calls=%async_computation.20 | async-start | bytes 5013504 | tf_op jit(solution)/shard_map/reduce_scatter | solution.py:160
  163.9 420.9 %reduce-scatter.26.cloned.1.call-start = ((), (), s32[]{:S(2)}) async-start(), calls=%async_computation.21 | async-start | bytes 5013504 | tf_op jit(solution)/shard_map/reduce_scatter | solution.py:166
  173.4 490.5 %reduce-scatter.20.cloned.1.call-start = ((), (), s32[]{:S(2)}) async-start(), calls=%async_computation.18 | async-start | bytes 1114112 | tf_op jit(solution)/shard_map/reduce_scatter | solution.py:163
  177.9 495.1 %reduce-scatter.16.cloned.1.call-start = ((), (), s32[]{:S(2)}) async-start(), calls=%async_computation.16 | async-start | bytes 3145728 | tf_op jit(solution)/shard_map/reduce_scatter | solution.py:141
  185.3 5.7 copy-start.8
  188.6 2.4 copy-start.9
  191.0 1.0 copy-start.10
  196.6 521.7 %reduce-scatter.12.cloned.1.call-start = ((), (), s32[]{:S(2)}) async-start(), calls=%async_computation.12 | async-start | bytes 3145728 | tf_op jit(solution)/shard_map/reduce_scatter | solution.py:103
  206.0 567.4 %reduce-scatter.18.cloned.1.call-start = ((), (), s32[]{:S(2)}) async-start(), calls=%async_computation.17 | async-start | bytes 3342336 | tf_op jit(solution)/shard_map/reduce_scatter | solution.py:154
  213.8 459.1 %copy-start.13 = (f32[1024]{0:T(1024)S(1)}, f32[1024]{0:T(1024)}, u32[]{:S(2)}) copy-start(f32[1024]{0:T(1024)} %param.13) | copy-start | bytes 12292
Sparse Core Ops, SparseCore 0:
  11.6 13.2 all-gather.4
  39.2 13.1 reduce-scatter.9
  57.3 11.8 all-gather.6
  70.7 11.7 all-gather.8
  125.0 13.2 reduce-scatter.13
  144.7 11.8 all-gather.10
  161.8 138.5 reduce-scatter.21
  306.4 136.6 reduce-scatter.23
  448.3 136.4 reduce-scatter.25
  587.0 76.8 reduce-scatter.19
  666.7 6.1 reduce-scatter.15
  675.1 10.7 reduce-scatter.11
  688.2 85.1 reduce-scatter.17
where the time goes:
time: 787 us; the launch traced here: 782 us
  waiting for transfers between devices  512 us (65%)
  matrix products  125 us (16%)
  blocking collectives  82.9 us (11%)
  other arithmetic  38.5 us (5%)
  between operations  14.6 us (2%)
    reduce_scatter x1, waiting for transfers between devices, local(): lax.psum_scatter(up_part.astype(jnp.bfloat16), 'dp', scatter_dimension=0,...  141 us
    reduce_scatter x1, waiting for transfers between devices, local(): lax.psum_scatter(down_part.astype(jnp.bfloat16), 'dp', scatter_dimension=...  140 us
    reduce_scatter x1, waiting for transfers between devices, local(): lax.psum_scatter(gate_part.astype(jnp.bfloat16), 'dp', scatter_dimension=...  86.5 us
    reduce_scatter x1, waiting for transfers between devices, local(): lax.psum_scatter(in_part.astype(jnp.bfloat16), 'dp', scatter_dimension=0,...  50 us
    dot_general x4, matrix products, dot_nt(): lax.dot_general(left, right, (((1,), (1,)), ((), ())), preferred_element_...  42.4 us
    psum x1, blocking collectives, local(): lax.psum((gain1_part, gain2_part), ('dp', 'tensor'))  41.7 us
    psum x1, blocking collectives, local(): kernel_grad = lax.psum(kernel_part, 'dp')  41.1 us
    reduce_scatter x1, waiting for transfers between devices, local(): lax.psum_scatter(out_part.astype(jnp.bfloat16), 'dp', scatter_dimension=1...  36.2 us
  transfers between devices with their start and end apart: 13, of which 10 were waited for; matrix products, arithmetic and copies ran while one was open for 13% of the time, Pallas kernels for 0%

commit v1 on v0

v1 whole, which is shorter than its diff:
```python
import jax
import jax.numpy as jnp
from jax import lax
from jax.sharding import PartitionSpec as P

EPSILON = 1e-06


def normalize(values):
    inverse = lax.rsqrt(jnp.mean(values * values, axis=-1, keepdims=True) + EPSILON)
    return (values * inverse, inverse)


def norm_back(grad_norm, unit_rows, inverse, scales):
    grad_unit = grad_norm * scales
    grad_in = inverse * (
        grad_unit - unit_rows * jnp.mean(grad_unit * unit_rows, axis=-1, keepdims=True)
    )
    return (grad_in, jnp.sum(grad_norm * unit_rows, axis=0))


def lagged(values, lag_steps):
    return jnp.roll(values, lag_steps, axis=0)


def leading(values, lag_steps):
    return jnp.roll(values, -lag_steps, axis=0)


def doc_mask(seg_row, lag_steps):
    same_doc = jnp.concatenate(
        [
            jnp.zeros((lag_steps,), jnp.int32),
            (seg_row[lag_steps:] == seg_row[:-lag_steps]).astype(jnp.int32),
        ]
    )
    return same_doc[:, None].astype(jnp.float32)


def dot_nt(left, right):
    return lax.dot_general(
        left, right, (((1,), (1,)), ((), ())), preferred_element_type=jnp.float32
    )


def dot_tn(left, right):
    return lax.dot_general(
        left, right, (((0,), (0,)), ((), ())), preferred_element_type=jnp.float32
    )


def rotate_rows(values, steps):
    twice = jnp.concatenate([values, values], axis=0)
    return lax.dynamic_slice_in_dim(twice, steps, values.shape[0], 0)


def swap(values):
    return lax.ppermute(values, "tensor", [(0, 1), (1, 0)])


def gather_rows(values):
    size = lax.axis_size("tensor")
    if size == 2:
        return jnp.concatenate([values, swap(values)], axis=0)
    whole = lax.all_gather(values, "tensor", axis=0, tiled=True)
    return rotate_rows(whole, lax.axis_index("tensor") * values.shape[0])


def sum_rows(product, own_rows, *operands):
    size = lax.axis_size("tensor")
    if size == 2:
        theirs = product(*(operand[own_rows:] for operand in operands))
        received = swap(theirs.astype(jnp.bfloat16))
        ours = product(*(operand[:own_rows] for operand in operands))
        return ours + received.astype(jnp.float32)
    total_rows = size * own_rows
    start = lax.axis_index("tensor") * own_rows
    ordered = rotate_rows(product(*operands), lax.rem(total_rows - start, total_rows))
    return lax.psum_scatter(
        ordered.astype(jnp.bfloat16), "tensor", scatter_dimension=0, tiled=True
    ).astype(jnp.float32)


def partners(bit):
    return [(i, i ^ (1 << bit)) for i in range(lax.axis_size("dp"))]


def dp_bits():
    return lax.axis_size("dp").bit_length() - 1


def dp_orders():
    bits = dp_bits()
    if bits == 4:
        return ((0, 2, 1, 3), (1, 2, 0, 3))
    return (tuple(range(bits)), tuple(reversed(range(bits))))


def halve(part, order):
    bits = dp_bits()
    me = lax.axis_index("dp")
    rows, columns = part.shape
    part = part.reshape((2,) * bits + (rows >> bits, columns))
    left = list(reversed(range(bits)))
    for bit in order:
        axis = left.index(bit)
        mine = lax.rem(me >> bit, 2)
        sent = lax.dynamic_index_in_dim(part, 1 - mine, axis, keepdims=False)
        kept = lax.dynamic_index_in_dim(part, mine, axis, keepdims=False)
        received = lax.ppermute(sent, "dp", partners(bit))
        part = kept.astype(jnp.float32) + received.astype(jnp.float32)
        left.remove(bit)
        if left:
            part = part.astype(jnp.bfloat16)
    return part


def reduce_dp(part):
    orders = dp_orders()
    width = part.shape[1] // len(orders)
    return jnp.concatenate(
        [halve(part[:, i * width : (i + 1) * width], order) for i, order in enumerate(orders)],
        axis=1,
    )


def sum_dp(values):
    for bit in range(dp_bits()):
        values = values + lax.ppermute(values, "dp", partners(bit))
    return values


def sum_gains(gains, local_ch):
    size = lax.axis_size("tensor")
    me = lax.axis_index("tensor")
    if size == 2:
        theirs = lax.dynamic_slice_in_dim(gains, (1 - me) * local_ch, local_ch, 1)
        ours = lax.dynamic_slice_in_dim(gains, me * local_ch, local_ch, 1)
        return ours + swap(theirs)
    return lax.dynamic_slice_in_dim(lax.psum(gains, "tensor"), me * local_ch, local_ch, 1)


def local(
    tokens,
    segments,
    norm1_gain,
    in_weight,
    conv_kernel,
    out_weight,
    norm2_gain,
    gate_weight,
    up_weight,
    down_weight,
    cotangent,
):
    own_rows, width = tokens.shape
    local_ch = conv_kernel.shape[1]
    taps = conv_kernel.shape[0]
    row_start = lax.axis_index("tensor") * own_rows
    seg_row = segments[0]
    inputs = tokens.astype(jnp.float32)
    unit1, inv1 = normalize(inputs)
    norm1 = (unit1 * norm1_gain).astype(jnp.bfloat16)
    norm1_all = gather_rows(norm1)
    cot_all = gather_rows(cotangent)
    projected = jnp.einsum("td,dkc->tkc", norm1_all, in_weight, preferred_element_type=jnp.float32)
    b_gate = projected[:, 0]
    c_gate = projected[:, 1]
    x_gate = projected[:, 2]
    gated = b_gate * x_gate
    conv_out = conv_kernel[taps - 1] * gated
    masks = []
    masked_lags = []
    for tap_index in range(taps - 1):
        lag_steps = taps - 1 - tap_index
        tap_mask = rotate_rows(doc_mask(seg_row, lag_steps), row_start)
        masked = lagged(gated, lag_steps) * tap_mask
        masks.append(tap_mask)
        masked_lags.append(masked)
        conv_out = conv_out + conv_kernel[tap_index] * masked
    mixer_act = (c_gate * conv_out).astype(jnp.bfloat16)
    mixer_out = sum_rows(
        lambda act: jnp.dot(act, out_weight, preferred_element_type=jnp.float32),
        own_rows,
        mixer_act,
    )
    middle = inputs + mixer_out
    unit2, inv2 = normalize(middle)
    norm2 = (unit2 * norm2_gain).astype(jnp.bfloat16)
    norm2_all = gather_rows(norm2)
    gate_val = jnp.dot(norm2_all, gate_weight, preferred_element_type=jnp.float32)
    up_val = jnp.dot(norm2_all, up_weight, preferred_element_type=jnp.float32)
    sigma = jax.nn.sigmoid(gate_val)
    silu_val = gate_val * sigma
    hidden = (silu_val * up_val).astype(jnp.bfloat16)
    cot_rows = cotangent.astype(jnp.float32)
    down_total = reduce_dp(dot_tn(cot_all, hidden).astype(jnp.bfloat16)).T
    ffn_out = sum_rows(
        lambda act: jnp.dot(act, down_weight, preferred_element_type=jnp.float32),
        own_rows,
        hidden,
    )
    mixed = (middle + ffn_out).astype(jnp.bfloat16)
    d_hidden = dot_nt(cot_all, down_weight)
    d_gate = (d_hidden * up_val * sigma * (1.0 + gate_val * (1.0 - sigma))).astype(jnp.bfloat16)
    d_up = (d_hidden * silu_val).astype(jnp.bfloat16)
    gate_total = reduce_dp(dot_tn(norm2_all, d_gate).astype(jnp.bfloat16))
    up_total = reduce_dp(dot_tn(norm2_all, d_up).astype(jnp.bfloat16))
    d_norm2 = sum_rows(
        lambda gate, up: dot_nt(gate, gate_weight) + dot_nt(up, up_weight),
        own_rows,
        d_gate,
        d_up,
    )
    d_mid_norm, gain2_part = norm_back(d_norm2, unit2, inv2, norm2_gain)
    d_middle = cot_rows + d_mid_norm
    d_middle_all = gather_rows(d_middle.astype(jnp.bfloat16))
    d_mixer = dot_nt(d_middle_all, out_weight)
    out_total = reduce_dp(dot_tn(d_middle_all, mixer_act).astype(jnp.bfloat16)).T
    d_conv = d_mixer * c_gate
    d_c = d_mixer * conv_out
    d_gated = conv_kernel[taps - 1] * d_conv
    kernel_rows = []
    for tap_index in range(taps - 1):
        lag_steps = taps - 1 - tap_index
        d_gated = d_gated + conv_kernel[tap_index] * leading(d_conv * masks[tap_index], lag_steps)
        kernel_rows.append(jnp.sum(d_conv * masked_lags[tap_index], axis=0))
    kernel_rows.append(jnp.sum(d_conv * gated, axis=0))
    kernel_part = jnp.stack(kernel_rows, axis=0)
    d_projected = jnp.concatenate([d_gated * x_gate, d_c, d_gated * b_gate], axis=1).astype(
        jnp.bfloat16
    )
    in_total = reduce_dp(dot_tn(norm1_all, d_projected).astype(jnp.bfloat16)).reshape(
        -1, 3, local_ch
    )
    in_flat = in_weight.reshape(width, -1)
    d_norm1 = sum_rows(lambda grad: dot_nt(grad, in_flat), own_rows, d_projected)
    d_in_norm, gain1_part = norm_back(d_norm1, unit1, inv1, norm1_gain)
    input_grad = d_middle + d_in_norm
    gains = sum_gains(jnp.stack([gain1_part, gain2_part]), local_ch)
    small = sum_dp(jnp.concatenate([gains, kernel_part], axis=0))
    return (
        mixed,
        input_grad,
        small[0],
        in_total,
        small[2:],
        out_total,
        small[1],
        gate_total,
        up_total,
        down_total,
    )


def solution(mesh):
    in_specs = (
        P(("dp", "tensor"), None),
        P("dp", None),
        P(),
        P(None, None, "tensor"),
        P(None, "tensor"),
        P("tensor", None),
        P(),
        P(None, "tensor"),
        P(None, "tensor"),
        P("tensor", None),
        P(("dp", "tensor"), None),
    )
    out_specs = (
        P(("dp", "tensor"), None),
        P(("dp", "tensor"), None),
        P("tensor"),
        P("dp", None, "tensor"),
        P(None, "tensor"),
        P("tensor", "dp"),
        P("tensor"),
        P("dp", "tensor"),
        P("dp", "tensor"),
        P("tensor", "dp"),
    )
    return jax.shard_map(local, mesh=mesh, in_specs=in_specs, out_specs=out_specs, check_vma=False)
```

time: 787 us -> 370 us (0.47)
  waiting for transfers between devices: 512 us -> 134 us
  blocking collectives: 82.9 us -> 0 us
  starting transfers between devices: 1.18 us -> 63.9 us
  local copies, waits for them, and re-layouts: 7.3 us -> 28.4 us
  other arithmetic: 38.5 us -> 22.6 us
  between operations: 14.6 us -> 2.3 us
  matrix products: 125 us -> 115 us
    reduce_scatter x9 -> x0, waiting for transfers between devices: 487 us -> none  [the longest x1 141 us: local(): lax.psum_scatter(up_part.astype(jnp.bfloat16), 'dp', scatter_dimension=0,...]
    ppermute x0 -> x53, waiting for transfers between devices: none -> 134 us  [the longest x40 117 us: halve(): received = lax.ppermute(sent, 'dp', partners(bit))]
    psum x2 -> x0, blocking collectives: 82.9 us -> none  [the longest x1 41.7 us: local(): lax.psum((gain1_part, gain2_part), ('dp', 'tensor'))]
    ppermute x0 -> x53, starting transfers between devices: none -> 63.9 us  [the longest x40 57.6 us: halve(): received = lax.ppermute(sent, 'dp', partners(bit))]
    all_gather x4 -> x0, waiting for transfers between devices: 24.3 us -> none  [the longest x1 13.1 us: local(): norm1_all = lax.all_gather(norm1, 'tensor', axis=0, tiled=True)]
    unnamed x34 -> x88, local copies, waits for them, and re-layouts: 5.85 us -> 14.1 us
    dot_general x4 -> x8, matrix products: 42.4 us -> 37.6 us  [dot_nt(): lax.dot_general(left, right, (((1,), (1,)), ((), ())), preferred_element_...]
    dot_general x4 -> x5, matrix products: 32.8 us -> 28.1 us  [dot_tn(): lax.dot_general(left, right, (((0,), (0,)), ((), ())), preferred_element_...]
  transfers between devices with their start and end apart: 13 -> 53, of which waited for: 10 -> 24; matrix products, arithmetic and copies ran while one was open for 13% -> 29% of each run, Pallas kernels for 0% -> 0%
where the time goes in v1:
time: 370 us; the launch traced here: 367 us
  waiting for transfers between devices  134 us (36%)
  matrix products  115 us (31%)
  starting transfers between devices  63.9 us (17%)
  local copies, waits for them, and re-layouts  28.4 us (8%)
  other arithmetic  22.6 us (6%)
    ppermute x40, waiting for transfers between devices, halve(): received = lax.ppermute(sent, 'dp', partners(bit))  117 us
    ppermute x40, starting transfers between devices, halve(): received = lax.ppermute(sent, 'dp', partners(bit))  57.6 us
    dot_general x8, matrix products, dot_nt(): lax.dot_general(left, right, (((1,), (1,)), ((), ())), preferred_element_...  37.6 us
    dot_general x5, matrix products, dot_tn(): lax.dot_general(left, right, (((0,), (0,)), ((), ())), preferred_element_...  28.1 us
    dot_general x1, matrix products, local(): jnp.dot(norm2_all, gate_weight, preferred_element_type=jnp.float32)  17.8 us
    unnamed x88, local copies, waits for them, and re-layouts  14.1 us
    ppermute x4, waiting for transfers between devices, sum_dp(): values = values + lax.ppermute(values, 'dp', partners(bit))  14 us
    dot_general x2, matrix products, local(): jnp.dot(act, down_weight, preferred_element_type=jnp.float32)  12.8 us
  transfers between devices with their start and end apart: 53, of which 24 were waited for; matrix products, arithmetic and copies ran while one was open for 29% of the time, Pallas kernels for 0%

profile of v1, /device:TPU:0, one launch (start us, length us, event | category | flops | bytes accessed | tf_op | source)
XLA Modules:
  0.0 366.5 jit_solution(16063645011949370667)
XLA Ops:
  0.7 1.6 fusion.29
  5.4 2.6 collective-permute-done
  8.0 5.6 %fusion.32 = f32[1024,3,512]{2,0,1:T(8,128)S(1)} fusion(bf16[1024,3,512]{2,0,1:T(8,128)(2,1)} %param.14, bf16[512,1024]{1,0:T(8,128)(2,1)} %collective-permute-done, bf16[512,1024]{1,0:T(8,128)(2,1)S(1)} %fusion.23), kind=kOutput, calls=%fused_computation.60 | convolution fusion | flops 3225419776 | bytes 11534336 | tf_op jit(solution)/shard_map/td,dkc->tkc/dot_general | solution.py:166
  14.2 2.1 copy-done.1
  16.3 2.7 multiply_convert_fusion.7
  20.0 1.7 convolution_convert_fusion.5
  22.1 4.7 %copy.39 = bf16[1024,3,512]{0,2,1:T(8,128)(2,1)} copy(bf16[1024,3,512]{2,0,1:T(8,128)(2,1)} %param.14) | data formatting | bytes 6291456 | tf_op args[3]
  29.8 3.0 multiply_reduce_fusion.5
  33.3 7.6 %fusion.105 = f32[1024,2304]{1,0:T(8,128)} fusion(bf16[1024,1024]{1,0:T(8,128)(2,1)S(1)} %constant_dynamic-update-slice_fusion, bf16[2304,1024]{1,0:T(8,128)(2,1)S(1)} %bitcast.368), kind=kOutput, calls=%fused_computation.269 | convolution fusion | flops 4831838208 | bytes 16252928 | tf_op jit(solution)/shard_map/dot_general | solution.py:41
  40.9 8.2 %fusion.93 = f32[1024,2304]{1,0:T(8,128)} fusion(bf16[1024,2304]{1,0:T(8,128)(2,1)S(1)} %bitcast.366, bf16[512,1024]{1,0:T(8,128)(2,1)S(1)} %collective-permute-done.2, bf16[512,1024]{1,0:T(8,128)(2,1)S(1)} %multiply_convert_fusion.6), kind=kOutput, calls=%fused_computation.259 | convolution fusion | flops 4836032512 | bytes 16252928 | tf_op jit(solution)/shard_map/dot_general | solution.py:192
  49.2 17.8 %multiply_convert_fusion.1 = (bf16[1024,2304]{1,0:T(8,128)(2,1)}, bf16[1024,2304]{1,0:T(8,128)(2,1)}, bf16[1024,2304]{1,0:T(8,128)(2,1)}) fusion(f32[1024,2304]{1,0:T(8,128)} %fusion.105, f32[1024,2304]{1,0:T(8,128)} %fusion.93, bf16[1024,2304]{1,0:T(8,128)(2,1)} %param.18, bf16[512,1024]{1,0:T(8,128)(2,1)S(1)} %collective-permute-done.2, ...), kind=kOutput, calls=%fused_computation.1 | convolution fusion | flops 4871421952 | bytes 39845888 | tf_op jit(solution)/shard_map/dot_general | solution.py:191
  66.9 5.8 %fusion.5 = f32[512,1024]{1,0:T(8,128)S(1)} fusion(bf16[1024,2304]{1,0:T(8,128)(2,1)} %param.19, bf16[1024,2304]{1,0:T(8,128)(2,1)} %get-tuple-element.33), kind=kOutput, calls=%fused_computation.17 | convolution fusion | flops 2415919104 | bytes 9175040 | tf_op jit(solution)/shard_map/dot_general | solution.py:41
  72.8 6.4 %fusion.9 = f32[512,1024]{1,0:T(8,128)} fusion(bf16[1024,2304]{1,0:T(8,128)(2,1)} %param.19, bf16[1024,2304]{1,0:T(8,128)(2,1)S(1)} %copy-done.29), kind=kOutput, calls=%fused_computation.21 | convolution fusion | flops 2415919104 | bytes 9175040 | tf_op jit(solution)/shard_map/dot_general | solution.py:41
  79.2 5.7 %convolution_convert_fusion = bf16[1024,2304]{1,0:T(8,128)(2,1)S(1)} fusion(bf16[1024,1024]{1,0:T(8,128)(2,1)S(1)} %copy-done.14, bf16[1024,2304]{1,0:T(8,128)(2,1)S(1)} %bitcast.372), kind=kOutput, calls=%fused_computation.5 | convolution fusion | flops 4834197504 | bytes 11534336 | tf_op jit(solution)/shard_map/dot_general | solution.py:47
  85.7 3.0 collective-permute-start.45
  89.0 1.6 collective-permute-start.49
  90.6 7.7 %convolution_convert_fusion.1 = bf16[1024,2304]{1,0:T(8,128)(2,1)S(1)} fusion(bf16[1024,2304]{1,0:T(8,128)(2,1)} %get-tuple-element.33, bf16[512,1024]{1,0:T(8,128)(2,1)S(1)} %copy-done.28, bf16[512,1024]{1,0:T(8,128)(2,1)S(1)} %copy-done.12), kind=kOutput, calls=%fused_computation.6 | convolution fusion | flops 4838391808 | bytes 11534336 | tf_op jit(solution)/shard_map/dot_general | solution.py:47
  102.3 7.7 %convolution_convert_fusion.2 = bf16[1024,2304]{1,0:T(8,128)(2,1)S(1)} fusion(bf16[1024,2304]{1,0:T(8,128)(2,1)} %get-tuple-element.32, bf16[512,1024]{1,0:T(8,128)(2,1)S(1)} %copy-done.28, bf16[512,1024]{1,0:T(8,128)(2,1)S(1)} %copy-done.12), kind=kOutput, calls=%fused_computation.7 | convolution fusion | flops 4838391808 | bytes 11534336 | tf_op jit(solution)/shard_map/dot_general | solution.py:47
  111.8 5.7 %add_convert_fusion = bf16[512,1024]{1,0:T(8,128)(2,1)S(1)} fusion(f32[512,1024]{1,0:T(8,128)S(1)} %fusion.5, bf16[1024,2304]{1,0:T(8,128)(2,1)} %param.18, bf16[1024,2304]{1,0:T(8,128)(2,1)} %get-tuple-element.32), kind=kOutput, calls=%fused_computation.73 | convolution fusion | flops 2416967680 | bytes 10223616 | tf_op jit(solution)/shard_map/dot_general | solution.py:41
  118.9 6.8 %fusion.51 = bf16[512,1024]{1,0:T(8,128)(2,1)} fusion(bf16[2304,1024]{1,0:T(8,128)(2,1)} %param.20, bf16[1024,2304]{1,0:T(8,128)(2,1)} %get-tuple-element.34), kind=kOutput, calls=%fused_computation.90 | convolution fusion | flops 2416443392 | bytes 8126464 | tf_op jit(solution)/shard_map/dot_general | solution.py:199
  127.2 6.0 %multiply_reduce_fusion.3 = (f32[1024]{0:T(1024)S(1)}, f32[512]{0:T(512)S(1)}, f32[512,1024]{1,0:T(8,128)S(1)}) fusion(f32[512,1024]{1,0:T(8,128)S(1)} %get-tuple-element.76, f32[512]{0:T(512)S(1)} %add_rsqrt_fusion, f32[1024]{0:T(1024)S(1)} %copy-done.22, bf16[512,1024]{1,0:T(8,128)(2,1)S(1)} %collective-permute-done.5, f32[512,1024]{1,0:T(8,128)S(1)} %copy-done.30, ...), kind=kOutput, calls=%fused_computation.65 | convolution fusion | flops 2420636160 | bytes 14430208 | tf_op jit(solution)/shard_map/dot_general | solution.py:41
  133.2 1.9 fusion.95
  136.6 4.1 %collective-permute-done.37 = bf16[2,2,2,64,1152]{4,3,0,2,1:T(8,128)(2,1)S(1)} collective-permute-done((bf16[2,2,2,64,1152]{4,3,0,2,1:T(8,128)(2,1)}, bf16[2,2,2,64,1152]{4,3,0,2,1:T(8,128)(2,1)S(1)}, u32[]{:S(2)}, u32[]{:S(2)}) %collective-permute-start.37) | collective-permute-done | bytes 1179680 | tf_op jit(solution)/shard_map/ppermute | solution.py:110
  141.2 2.0 collective-permute-done.41
  143.2 1.6 collective-permute-start.46
  145.1 20.4 %collective-permute-done.29 = bf16[2,2,2,64,1152]{4,3,0,2,1:T(8,128)(2,1)S(1)} collective-permute-done((bf16[2,2,2,64,1152]{4,3,0,2,1:T(8,128)(2,1)}, bf16[2,2,2,64,1152]{4,3,0,2,1:T(8,128)(2,1)S(1)}, u32[]{:S(2)}, u32[]{:S(2)}) %collective-permute-start.29) | collective-permute-done | bytes 1179680 | tf_op jit(solution)/shard_map/ppermute | solution.py:110
  165.5 1.8 collective-permute-start.50
  170.4 11.3 %collective-permute-done.50 = bf16[2,2,64,1152]{3,2,0,1:T(8,128)(2,1)S(1)} collective-permute-done((bf16[2,2,64,1152]{3,2,0,1:T(8,128)(2,1)S(1)}, bf16[2,2,64,1152]{3,2,0,1:T(8,128)(2,1)S(1)}, u32[]{:S(2)}, u32[]{:S(2)}) %collective-permute-start.50) | collective-permute-done | bytes 589856 | tf_op jit(solution)/shard_map/ppermute | solution.py:110
  181.7 1.8 collective-permute-start.30
  183.7 10.6 %collective-permute-done.38 = bf16[2,2,64,1152]{3,2,0,1:T(8,128)(2,1)S(1)} collective-permute-done((bf16[2,2,64,1152]{3,2,0,1:T(8,128)(2,1)S(1)}, bf16[2,2,64,1152]{3,2,0,1:T(8,128)(2,1)S(1)}, u32[]{:S(2)}, u32[]{:S(2)}) %collective-permute-start.38) | collective-permute-done | bytes 589856 | tf_op jit(solution)/shard_map/ppermute | solution.py:110
  194.3 1.8 collective-permute-start.34
  196.3 10.7 %collective-permute-done.42 = bf16[2,2,64,1152]{3,2,0,1:T(8,128)(2,1)S(1)} collective-permute-done((bf16[2,2,64,1152]{3,2,0,1:T(8,128)(2,1)S(1)}, bf16[2,2,64,1152]{3,2,0,1:T(8,128)(2,1)S(1)}, u32[]{:S(2)}, u32[]{:S(2)}) %collective-permute-start.42) | collective-permute-done | bytes 589856 | tf_op jit(solution)/shard_map/ppermute | solution.py:110
  207.0 1.8 collective-permute-start.47
  209.0 10.6 %collective-permute-done.30 = bf16[2,2,64,1152]{3,2,0,1:T(8,128)(2,1)S(1)} collective-permute-done((bf16[2,2,64,1152]{3,2,0,1:T(8,128)(2,1)S(1)}, bf16[2,2,64,1152]{3,2,0,1:T(8,128)(2,1)S(1)}, u32[]{:S(2)}, u32[]{:S(2)}) %collective-permute-start.30) | collective-permute-done | bytes 589856 | tf_op jit(solution)/shard_map/ppermute | solution.py:110
  219.6 1.8 collective-permute-start.51
  221.6 9.3 %collective-permute-done.34 = bf16[2,2,64,1152]{3,2,0,1:T(8,128)(2,1)S(1)} collective-permute-done((bf16[2,2,64,1152]{3,2,0,1:T(8,128)(2,1)S(1)}, bf16[2,2,64,1152]{3,2,0,1:T(8,128)(2,1)S(1)}, u32[]{:S(2)}, u32[]{:S(2)}) %collective-permute-start.34) | collective-permute-done | bytes 589856 | tf_op jit(solution)/shard_map/ppermute | solution.py:110
  232.5 1.6 collective-permute-start.43
  234.9 5.9 %collective-permute-done.39 = bf16[2,64,1152]{2,1,0:T(8,128)(2,1)S(1)} collective-permute-done((bf16[2,64,1152]{2,1,0:T(8,128)(2,1)S(1)}, bf16[2,64,1152]{2,1,0:T(8,128)(2,1)S(1)}, u32[]{:S(2)}, u32[]{:S(2)}) %collective-permute-start.39) | collective-permute-done | bytes 294944 | tf_op jit(solution)/shard_map/ppermute | solution.py:110
  243.0 2.5 collective-permute-start.48
  248.2 2.6 collective-permute-start.40
  251.4 2.1 multiply_reduce_fusion.2
  260.3 5.6 %convolution_convert_fusion.3 = bf16[1024,1536]{1,0:T(8,128)(2,1)S(1)} fusion(bf16[512,1024]{1,0:T(8,128)(2,1)} %collective-permute-done, bf16[512,1024]{1,0:T(8,128)(2,1)S(1)} %copy-done.10, bf16[1024,512]{1,0:T(8,128)(2,1)S(1)} %multiply_convert_fusion.3, bf16[1024,512]{1,0:T(8,128)(2,1)S(1)} %get-tuple-element.57, bf16[1024,512]{1,0:T(8,128)(2,1)S(1)} %get-tuple-element.28), kind=kOutput, calls=%fused_computation.8 | convolution fusion | flops 3236429824 | bytes 8388608 | tf_op jit(solution)/shard_map/dot_general | solution.py:47
  266.4 1.7 copy-done.5
  268.0 1.8 fusion.48
  270.1 2.6 collective-permute-start.32
  277.1 1.6 collective-permute-start.25
  285.5 2.4 collective-permute-start.22
  288.0 3.5 collective-permute-done.22
  292.9 3.4 collective-permute-done.26
  297.5 4.5 %collective-permute-done.23 = bf16[2,64,256]{2,1,0:T(8,128)(2,1)S(1)} collective-permute-done((bf16[2,64,256]{2,1,0:T(8,128)(2,1)S(1)}, bf16[2,64,256]{2,1,0:T(8,128)(2,1)S(1)}, u32[]{:S(2)}, u32[]{:S(2)}) %collective-permute-start.23) | collective-permute-done | bytes 65568 | tf_op jit(solution)/shard_map/ppermute | solution.py:110
  302.0 1.6 collective-permute-start.27
  303.6 2.6 collective-permute-done.27
  307.6 3.8 %collective-permute-done.24 = bf16[64,256]{1,0:T(8,128)(2,1)S(1)} collective-permute-done((bf16[64,256]{1,0:T(8,128)(2,1)S(1)}, bf16[64,256]{1,0:T(8,128)(2,1)S(1)}, u32[]{:S(2)}, u32[]{:S(2)}) %collective-permute-start.24) | collective-permute-done | bytes 32800 | tf_op jit(solution)/shard_map/ppermute | solution.py:110
  312.5 3.7 %collective-permute-done.28 = bf16[64,256]{1,0:T(8,128)(2,1)S(1)} collective-permute-done((bf16[64,256]{1,0:T(8,128)(2,1)S(1)}, bf16[64,256]{1,0:T(8,128)(2,1)S(1)}, u32[]{:S(2)}, u32[]{:S(2)}) %collective-permute-start.28) | collective-permute-done | bytes 32800 | tf_op jit(solution)/shard_map/ppermute | solution.py:110
  317.2 2.2 fusion.28
  320.8 1.5 collective-permute-start.9
  322.5 2.1 collective-permute-done.9
  329.4 10.5 %collective-permute-done.11 = f32[5,512]{1,0:T(8,128)S(1)} collective-permute-done((f32[5,512]{1,0:T(8,128)S(1)}, f32[5,512]{1,0:T(8,128)S(1)}, u32[]{:S(2)}, u32[]{:S(2)}) %collective-permute-start.11) | collective-permute-done | bytes 10272 | tf_op jit(solution)/shard_map/ppermute | solution.py:129
  341.1 6.0 %fusion.27 = (f32[512,1024]{1,0:T(8,128)}, bf16[512,1024]{1,0:T(8,128)(2,1)}) fusion(bf16[512,1024]{1,0:T(8,128)(2,1)S(1)} %copy-done.3, f32[512,1024]{1,0:T(8,128)S(1)} %get-tuple-element.78, f32[512]{0:T(512)S(1)} %broadcast_multiply_fusion.2, f32[1024]{0:T(1024)S(1)} %copy-done.26, f32[512]{0:T(512)S(1)} %copy-done.24, ...), kind=kOutput, calls=%fused_computation.45 | convolution fusion | flops 2425356288 | bytes 19677184 | tf_op jit(solution)/shard_map/dot_general | solution.py:199
  348.5 1.6 collective-permute-start.15
  350.2 2.0 collective-permute-start.19
  352.1 2.7 collective-permute-done.15
  354.9 1.7 collective-permute-start.16
  358.0 6.4 %collective-permute-done.16 = bf16[64,768]{1,0:T(8,128)(2,1)S(1)} collective-permute-done((bf16[64,768]{1,0:T(8,128)(2,1)S(1)}, bf16[64,768]{1,0:T(8,128)(2,1)S(1)}, u32[]{:S(2)}, u32[]{:S(2)}) %collective-permute-start.16) | collective-permute-done | bytes 98336 | tf_op jit(solution)/shard_map/ppermute | solution.py:110
  (293 shorter events, 68.5 us)
Async XLA Ops:
  0.6 19.4 %copy-start = (bf16[512,1024]{1,0:T(8,128)(2,1)S(1)}, bf16[512,1024]{1,0:T(8,128)(2,1)}, u32[]{:S(2)}) copy-start(bf16[512,1024]{1,0:T(8,128)(2,1)} %param.16) | copy-start | bytes 3145732
  4.4 3.6 collective-permute-start
  4.9 23.3 %collective-permute-start.4 = (bf16[512,1024]{1,0:T(8,128)(2,1)}, bf16[512,1024]{1,0:T(8,128)(2,1)}, u32[]{:S(2)}, u32[]{:S(2)}) collective-permute-start(bf16[512,1024]{1,0:T(8,128)(2,1)} %param.21), channel_id=1, source_target_pairs={{0,1},{1,0},{2,3},{3,2},{4,5},{5,4},{6,7},{7,6},{8,9},{9,8},{10,11... | collective-permute-start | bytes 3145736 | tf_op jit(solution)/shard_map/ppermute | solution.py:58
  21.7 8.1 %collective-permute-start.1 = (bf16[512,1024]{1,0:T(8,128)(2,1)}, bf16[512,1024]{1,0:T(8,128)(2,1)}, u32[]{:S(2)}, u32[]{:S(2)}) collective-permute-start(bf16[512,1024]{1,0:T(8,128)(2,1)} %convolution_convert_fusion.5), channel_id=1, source_target_pairs={{0,1},{1,0},{2,3},{3,2},{4,5},{5,4},{6,7},{7,6},{8,9},{9,8},{10,11... | collective-permute-start | bytes 3145736 | tf_op jit(solution)/shard_map/ppermute | solution.py:58
  33.1 16.1 %copy-start.11 = (bf16[512,1024]{1,0:T(8,128)(2,1)}, bf16[512,1024]{1,0:T(8,128)(2,1)S(1)}, u32[]{:S(2)}) copy-start(bf16[512,1024]{1,0:T(8,128)(2,1)S(1)} %multiply_convert_fusion.6) | copy-start | bytes 3145732
  33.1 7.8 %collective-permute-start.2 = (bf16[512,1024]{1,0:T(8,128)(2,1)S(1)}, bf16[512,1024]{1,0:T(8,128)(2,1)S(1)}, u32[]{:S(2)}, u32[]{:S(2)}) collective-permute-start(bf16[512,1024]{1,0:T(8,128)(2,1)S(1)} %multiply_convert_fusion.6), channel_id=1, source_target_pairs={{0,1},{1,0},{2,3},{3,2},{4,5},{5,4},{6,7},{7,6},{8,9},{9,8},{10,11... | collective-permute-start | bytes 3145736 | tf_op jit(solution)/shard_map/ppermute | solution.py:58
  85.7 49.4 %collective-permute-start.45 = (bf16[2,2,2,64,1152]{4,3,0,2,1:T(8,128)(2,1)S(1)}, bf16[2,2,2,64,1152]{4,3,0,2,1:T(8,128)(2,1)S(1)}, u32[]{:S(2)}, u32[]{:S(2)}) collective-permute-start(bf16[2,2,2,64,1152]{4,3,0,2,1:T(8,128)(2,1)S(1)} %bitcast.334), channel_id=1, source_target_pairs={{0,2},{2,0},{4,6},{6,4},{8,10},{10,8},{12,14},{14,12},{16,18},{18,... | collective-permute-start | bytes 3538952 | tf_op jit(solution)/shard_map/ppermute | solution.py:110
  89.0 47.2 %collective-permute-start.49 = (bf16[2,2,2,64,1152]{4,3,0,2,1:T(8,128)(2,1)S(1)}, bf16[2,2,2,64,1152]{4,3,0,2,1:T(8,128)(2,1)S(1)}, u32[]{:S(2)}, u32[]{:S(2)}) collective-permute-start(bf16[2,2,2,64,1152]{4,3,0,2,1:T(8,128)(2,1)S(1)} %bitcast.332), channel_id=1, source_target_pairs={{0,4},{2,6},{4,0},{6,2},{8,12},{10,14},{12,8},{14,10},{16,20},{18,... | collective-permute-start | bytes 3538952 | tf_op jit(solution)/shard_map/ppermute | solution.py:110
  100.0 40.6 %collective-permute-start.37 = (bf16[2,2,2,64,1152]{4,3,0,2,1:T(8,128)(2,1)}, bf16[2,2,2,64,1152]{4,3,0,2,1:T(8,128)(2,1)S(1)}, u32[]{:S(2)}, u32[]{:S(2)}) collective-permute-start(bf16[2,2,2,64,1152]{4,3,0,2,1:T(8,128)(2,1)} %bitcast.303), channel_id=1, source_target_pairs={{0,2},{2,0},{4,6},{6,4},{8,10},{10,8},{12,14},{14,12},{16,18},{18,... | collective-permute-start | bytes 3538952 | tf_op jit(solution)/shard_map/ppermute | solution.py:110
  100.9 42.3 %collective-permute-start.41 = (bf16[2,2,2,64,1152]{4,3,0,2,1:T(8,128)(2,1)S(1)}, bf16[2,2,2,64,1152]{4,3,0,2,1:T(8,128)(2,1)S(1)}, u32[]{:S(2)}, u32[]{:S(2)}) collective-permute-start(bf16[2,2,2,64,1152]{4,3,0,2,1:T(8,128)(2,1)S(1)} %bitcast.333), channel_id=1, source_target_pairs={{0,4},{2,6},{4,0},{6,2},{8,12},{10,14},{12,8},{14,10},{16,20},{18,... | collective-permute-start | bytes 3538952 | tf_op jit(solution)/shard_map/ppermute | solution.py:110
  117.5 8.2 %collective-permute-start.5 = (bf16[512,1024]{1,0:T(8,128)(2,1)S(1)}, bf16[512,1024]{1,0:T(8,128)(2,1)S(1)}, u32[]{:S(2)}, u32[]{:S(2)}) collective-permute-start(bf16[512,1024]{1,0:T(8,128)(2,1)S(1)} %add_convert_fusion), channel_id=1, source_target_pairs={{0,1},{1,0},{2,3},{3,2},{4,5},{5,4},{6,7},{7,6},{8,9},{9,8},{10,11... | collective-permute-start | bytes 3145736 | tf_op jit(solution)/shard_map/ppermute | solution.py:58
  125.7 39.8 %collective-permute-start.29 = (bf16[2,2,2,64,1152]{4,3,0,2,1:T(8,128)(2,1)}, bf16[2,2,2,64,1152]{4,3,0,2,1:T(8,128)(2,1)S(1)}, u32[]{:S(2)}, u32[]{:S(2)}) collective-permute-start(bf16[2,2,2,64,1152]{4,3,0,2,1:T(8,128)(2,1)} %bitcast.305), channel_id=1, source_target_pairs={{0,2},{2,0},{4,6},{6,4},{8,10},{10,8},{12,14},{14,12},{16,18},{18,... | collective-permute-start | bytes 3538952 | tf_op jit(solution)/shard_map/ppermute | solution.py:110
  135.1 32.5 %collective-permute-start.33 = (bf16[2,2,2,64,1152]{4,3,0,2,1:T(8,128)(2,1)}, bf16[2,2,2,64,1152]{4,3,0,2,1:T(8,128)(2,1)S(1)}, u32[]{:S(2)}, u32[]{:S(2)}) collective-permute-start(bf16[2,2,2,64,1152]{4,3,0,2,1:T(8,128)(2,1)} %bitcast.304), channel_id=1, source_target_pairs={{0,4},{2,6},{4,0},{6,2},{8,12},{10,14},{12,8},{14,10},{16,20},{18,... | collective-permute-start | bytes 3538952 | tf_op jit(solution)/shard_map/ppermute | solution.py:110
  136.2 204.9 %collective-permute-start.3 = (bf16[512,1024]{1,0:T(8,128)(2,1)}, bf16[512,1024]{1,0:T(8,128)(2,1)}, u32[]{:S(2)}, u32[]{:S(2)}) collective-permute-start(bf16[512,1024]{1,0:T(8,128)(2,1)} %fusion.51), channel_id=1, source_target_pairs={{0,1},{1,0},{2,3},{3,2},{4,5},{5,4},{6,7},{7,6},{8,9},{9,8},{10,11... | collective-permute-start | bytes 3145736 | tf_op jit(solution)/shard_map/ppermute | solution.py:58
  140.7 110.2 %collective-permute-start.6 = (bf16[512,1024]{1,0:T(8,128)(2,1)S(1)}, bf16[512,1024]{1,0:T(8,128)(2,1)S(1)}, u32[]{:S(2)}, u32[]{:S(2)}) collective-permute-start(bf16[512,1024]{1,0:T(8,128)(2,1)S(1)} %fusion.95), channel_id=1, source_target_pairs={{0,1},{1,0},{2,3},{3,2},{4,5},{5,4},{6,7},{7,6},{8,9},{9,8},{10,11... | collective-permute-start | bytes 3145736 | tf_op jit(solution)/shard_map/ppermute | solution.py:58
  143.2 26.2 %collective-permute-start.46 = (bf16[2,2,64,1152]{3,2,0,1:T(8,128)(2,1)S(1)}, bf16[2,2,64,1152]{3,2,0,1:T(8,128)(2,1)S(1)}, u32[]{:S(2)}, u32[]{:S(2)}) collective-permute-start(bf16[2,2,64,1152]{3,2,0,1:T(8,128)(2,1)S(1)} %dynamic-slice_bitcast_fusion.1), channel_id=1, source_target_pairs={{0,8},{2,10},{4,12},{6,14},{8,0},{10,2},{12,4},{14,6},{16,24},{18,... | collective-permute-start | bytes 1769480 | tf_op jit(solution)/shard_map/ppermute | solution.py:110
  165.5 16.2 %collective-permute-start.50 = (bf16[2,2,64,1152]{3,2,0,1:T(8,128)(2,1)S(1)}, bf16[2,2,64,1152]{3,2,0,1:T(8,128)(2,1)S(1)}, u32[]{:S(2)}, u32[]{:S(2)}) collective-permute-start(bf16[2,2,64,1152]{3,2,0,1:T(8,128)(2,1)S(1)} %dynamic-slice_bitcast_fusion), channel_id=1, source_target_pairs={{0,8},{2,10},{4,12},{6,14},{8,0},{10,2},{12,4},{14,6},{16,24},{18,... | collective-permute-start | bytes 1769480 | tf_op jit(solution)/shard_map/ppermute | solution.py:110
  167.6 26.8 %collective-permute-start.38 = (bf16[2,2,64,1152]{3,2,0,1:T(8,128)(2,1)S(1)}, bf16[2,2,64,1152]{3,2,0,1:T(8,128)(2,1)S(1)}, u32[]{:S(2)}, u32[]{:S(2)}) collective-permute-start(bf16[2,2,64,1152]{3,2,0,1:T(8,128)(2,1)S(1)} %dynamic-slice_bitcast_fusion.3), channel_id=1, source_target_pairs={{0,8},{2,10},{4,12},{6,14},{8,0},{10,2},{12,4},{14,6},{16,24},{18,... | collective-permute-start | bytes 1769480 | tf_op jit(solution)/shard_map/ppermute | solution.py:110
  169.4 37.6 %collective-permute-start.42 = (bf16[2,2,64,1152]{3,2,0,1:T(8,128)(2,1)S(1)}, bf16[2,2,64,1152]{3,2,0,1:T(8,128)(2,1)S(1)}, u32[]{:S(2)}, u32[]{:S(2)}) collective-permute-start(bf16[2,2,64,1152]{3,2,0,1:T(8,128)(2,1)S(1)} %dynamic-slice_bitcast_fusion.2), channel_id=1, source_target_pairs={{0,8},{2,10},{4,12},{6,14},{8,0},{10,2},{12,4},{14,6},{16,24},{18,... | collective-permute-start | bytes 1769480 | tf_op jit(solution)/shard_map/ppermute | solution.py:110
  181.7 37.9 %collective-permute-start.30 = (bf16[2,2,64,1152]{3,2,0,1:T(8,128)(2,1)S(1)}, bf16[2,2,64,1152]{3,2,0,1:T(8,128)(2,1)S(1)}, u32[]{:S(2)}, u32[]{:S(2)}) collective-permute-start(bf16[2,2,64,1152]{3,2,0,1:T(8,128)(2,1)S(1)} %dynamic-slice_bitcast_fusion.5), channel_id=1, source_target_pairs={{0,8},{2,10},{4,12},{6,14},{8,0},{10,2},{12,4},{14,6},{16,24},{18,... | collective-permute-start | bytes 1769480 | tf_op jit(solution)/shard_map/ppermute | solution.py:110
  183.7 67.7 %slice-start = ((s8[6291456]{0:T(1024)(128)(4,1)}), s8[4194304]{0:T(1024)(128)(4,1)S(1)}, s32[]{:S(2)}) async-start(s8[6291456]{0:T(1024)(128)(4,1)} %bitcast.317), calls=%async_computation | async-start | bytes 8388608
  194.3 36.5 %collective-permute-start.34 = (bf16[2,2,64,1152]{3,2,0,1:T(8,128)(2,1)S(1)}, bf16[2,2,64,1152]{3,2,0,1:T(8,128)(2,1)S(1)}, u32[]{:S(2)}, u32[]{:S(2)}) collective-permute-start(bf16[2,2,64,1152]{3,2,0,1:T(8,128)(2,1)S(1)} %dynamic-slice_bitcast_fusion.4), channel_id=1, source_target_pairs={{0,8},{2,10},{4,12},{6,14},{8,0},{10,2},{12,4},{14,6},{16,24},{18,... | collective-permute-start | bytes 1769480 | tf_op jit(solution)/shard_map/ppermute | solution.py:110
  207.0 25.6 %collective-permute-start.47 = (bf16[2,64,1152]{2,1,0:T(8,128)(2,1)S(1)}, bf16[2,64,1152]{2,1,0:T(8,128)(2,1)S(1)}, u32[]{:S(2)}, u32[]{:S(2)}) collective-permute-start(bf16[2,64,1152]{2,1,0:T(8,128)(2,1)S(1)} %dynamic-slice_bitcast_fusion.9), channel_id=1, source_target_pairs={{0,4},{2,6},{4,0},{6,2},{8,12},{10,14},{12,8},{14,10},{16,20},{18,... | collective-permute-start | bytes 884744 | tf_op jit(solution)/shard_map/ppermute | solution.py:110
  219.6 14.6 %collective-permute-start.51 = (bf16[2,64,1152]{2,1,0:T(8,128)(2,1)S(1)}, bf16[2,64,1152]{2,1,0:T(8,128)(2,1)S(1)}, u32[]{:S(2)}, u32[]{:S(2)}) collective-permute-start(bf16[2,64,1152]{2,1,0:T(8,128)(2,1)S(1)} %dynamic-slice_bitcast_fusion.8), channel_id=1, source_target_pairs={{0,2},{2,0},{4,6},{6,4},{8,10},{10,8},{12,14},{14,12},{16,18},{18,... | collective-permute-start | bytes 884744 | tf_op jit(solution)/shard_map/ppermute | solution.py:110
  221.6 29.8 %slice-start.1 = ((s8[6291456]{0:T(1024)(128)(4,1)}), s8[2097152]{0:T(1024)(128)(4,1)S(1)}, s32[]{:S(2)}) async-start(s8[6291456]{0:T(1024)(128)(4,1)} %bitcast.317), calls=%async_computation.1 | async-start | bytes 4194304
  230.9 9.9 %collective-permute-start.39 = (bf16[2,64,1152]{2,1,0:T(8,128)(2,1)S(1)}, bf16[2,64,1152]{2,1,0:T(8,128)(2,1)S(1)}, u32[]{:S(2)}, u32[]{:S(2)}) collective-permute-start(bf16[2,64,1152]{2,1,0:T(8,128)(2,1)S(1)} %dynamic-slice_bitcast_fusion.11), channel_id=1, source_target_pairs={{0,4},{2,6},{4,0},{6,2},{8,12},{10,14},{12,8},{14,10},{16,20},{18,... | collective-permute-start | bytes 884744 | tf_op jit(solution)/shard_map/ppermute | solution.py:110
  232.5 10.5 %collective-permute-start.43 = (bf16[2,64,1152]{2,1,0:T(8,128)(2,1)S(1)}, bf16[2,64,1152]{2,1,0:T(8,128)(2,1)S(1)}, u32[]{:S(2)}, u32[]{:S(2)}) collective-permute-start(bf16[2,64,1152]{2,1,0:T(8,128)(2,1)S(1)} %dynamic-slice_bitcast_fusion.10), channel_id=1, source_target_pairs={{0,2},{2,0},{4,6},{6,4},{8,10},{10,8},{12,14},{14,12},{16,18},{18,... | collective-permute-start | bytes 884744 | tf_op jit(solution)/shard_map/ppermute | solution.py:110
  234.2 12.8 %collective-permute-start.31 = (bf16[2,64,1152]{2,1,0:T(8,128)(2,1)S(1)}, bf16[2,64,1152]{2,1,0:T(8,128)(2,1)S(1)}, u32[]{:S(2)}, u32[]{:S(2)}) collective-permute-start(bf16[2,64,1152]{2,1,0:T(8,128)(2,1)S(1)} %dynamic-slice_bitcast_fusion.13), channel_id=1, source_target_pairs={{0,4},{2,6},{4,0},{6,2},{8,12},{10,14},{12,8},{14,10},{16,20},{18,... | collective-permute-start | bytes 884744 | tf_op jit(solution)/shard_map/ppermute | solution.py:110
  240.8 7.3 %collective-permute-start.35 = (bf16[2,64,1152]{2,1,0:T(8,128)(2,1)S(1)}, bf16[2,64,1152]{2,1,0:T(8,128)(2,1)S(1)}, u32[]{:S(2)}, u32[]{:S(2)}) collective-permute-start(bf16[2,64,1152]{2,1,0:T(8,128)(2,1)S(1)} %dynamic-slice_bitcast_fusion.12), channel_id=1, source_target_pairs={{0,2},{2,0},{4,6},{6,4},{8,10},{10,8},{12,14},{14,12},{16,18},{18,... | collective-permute-start | bytes 884744 | tf_op jit(solution)/shard_map/ppermute | solution.py:110
  243.0 27.0 %collective-permute-start.48 = (bf16[64,1152]{1,0:T(8,128)(2,1)}, bf16[64,1152]{1,0:T(8,128)(2,1)}, u32[]{:S(2)}, u32[]{:S(2)}) collective-permute-start(bf16[64,1152]{1,0:T(8,128)(2,1)} %dynamic-slice_bitcast_fusion.17), channel_id=1, source_target_pairs={{0,16},{2,18},{4,20},{6,22},{8,24},{10,26},{12,28},{14,30},{16,0},... | collective-permute-start | bytes 442376 | tf_op jit(solution)/shard_map/ppermute | solution.py:110
  247.0 26.6 %collective-permute-start.52 = (bf16[64,1152]{1,0:T(8,128)(2,1)}, bf16[64,1152]{1,0:T(8,128)(2,1)}, u32[]{:S(2)}, u32[]{:S(2)}) collective-permute-start(bf16[64,1152]{1,0:T(8,128)(2,1)} %dynamic-slice_bitcast_fusion.16), channel_id=1, source_target_pairs={{0,16},{2,18},{4,20},{6,22},{8,24},{10,26},{12,28},{14,30},{16,0},... | collective-permute-start | bytes 442376 | tf_op jit(solution)/shard_map/ppermute | solution.py:110
  248.2 26.9 %collective-permute-start.40 = (bf16[64,1152]{1,0:T(8,128)(2,1)}, bf16[64,1152]{1,0:T(8,128)(2,1)}, u32[]{:S(2)}, u32[]{:S(2)}) collective-permute-start(bf16[64,1152]{1,0:T(8,128)(2,1)} %dynamic-slice_bitcast_fusion.19), channel_id=1, source_target_pairs={{0,16},{2,18},{4,20},{6,22},{8,24},{10,26},{12,28},{14,30},{16,0},... | collective-permute-start | bytes 442376 | tf_op jit(solution)/shard_map/ppermute | solution.py:110
  250.9 26.2 %collective-permute-start.44 = (bf16[64,1152]{1,0:T(8,128)(2,1)}, bf16[64,1152]{1,0:T(8,128)(2,1)}, u32[]{:S(2)}, u32[]{:S(2)}) collective-permute-start(bf16[64,1152]{1,0:T(8,128)(2,1)} %dynamic-slice_bitcast_fusion.18), channel_id=1, source_target_pairs={{0,16},{2,18},{4,20},{6,22},{8,24},{10,26},{12,28},{14,30},{16,0},... | collective-permute-start | bytes 442376 | tf_op jit(solution)/shard_map/ppermute | solution.py:110
  270.1 10.9 %collective-permute-start.32 = (bf16[64,1152]{1,0:T(8,128)(2,1)S(1)}, bf16[64,1152]{1,0:T(8,128)(2,1)S(1)}, u32[]{:S(2)}, u32[]{:S(2)}) collective-permute-start(bf16[64,1152]{1,0:T(8,128)(2,1)S(1)} %dynamic-slice_bitcast_fusion.21), channel_id=1, source_target_pairs={{0,16},{2,18},{4,20},{6,22},{8,24},{10,26},{12,28},{14,30},{16,0},... | collective-permute-start | bytes 442376 | tf_op jit(solution)/shard_map/ppermute | solution.py:110
  273.6 9.3 %collective-permute-start.36 = (bf16[64,1152]{1,0:T(8,128)(2,1)S(1)}, bf16[64,1152]{1,0:T(8,128)(2,1)S(1)}, u32[]{:S(2)}, u32[]{:S(2)}) collective-permute-start(bf16[64,1152]{1,0:T(8,128)(2,1)S(1)} %dynamic-slice_bitcast_fusion.20), channel_id=1, source_target_pairs={{0,16},{2,18},{4,20},{6,22},{8,24},{10,26},{12,28},{14,30},{16,0},... | collective-permute-start | bytes 442376 | tf_op jit(solution)/shard_map/ppermute | solution.py:110
  275.0 10.3 %collective-permute-start.21 = (bf16[2,2,2,64,256]{4,3,0,2,1:T(8,128)(2,1)S(1)}, bf16[2,2,2,64,256]{4,3,0,2,1:T(8,128)(2,1)S(1)}, u32[]{:S(2)}, u32[]{:S(2)}) collective-permute-start(bf16[2,2,2,64,256]{4,3,0,2,1:T(8,128)(2,1)S(1)} %bitcast.339), channel_id=1, source_target_pairs={{0,2},{2,0},{4,6},{6,4},{8,10},{10,8},{12,14},{14,12},{16,18},{18,... | collective-permute-start | bytes 786440 | tf_op jit(solution)/shard_map/ppermute | solution.py:110
  277.1 8.3 %collective-permute-start.25 = (bf16[2,2,2,64,256]{4,3,0,2,1:T(8,128)(2,1)S(1)}, bf16[2,2,2,64,256]{4,3,0,2,1:T(8,128)(2,1)S(1)}, u32[]{:S(2)}, u32[]{:S(2)}) collective-permute-start(bf16[2,2,2,64,256]{4,3,0,2,1:T(8,128)(2,1)S(1)} %bitcast.338), channel_id=1, source_target_pairs={{0,4},{2,6},{4,0},{6,2},{8,12},{10,14},{12,8},{14,10},{16,20},{18,... | collective-permute-start | bytes 786440 | tf_op jit(solution)/shard_map/ppermute | solution.py:110
  281.0 35.9 %collective-permute-start.13 = (bf16[2,2,2,64,768]{4,3,0,2,1:T(8,128)(2,1)S(1)}, bf16[2,2,2,64,768]{4,3,0,2,1:T(8,128)(2,1)S(1)}, u32[]{:S(2)}, u32[]{:S(2)}) collective-permute-start(bf16[2,2,2,64,768]{4,3,0,2,1:T(8,128)(2,1)S(1)} %bitcast.336), channel_id=1, source_target_pairs={{0,2},{2,0},{4,6},{6,4},{8,10},{10,8},{12,14},{14,12},{16,18},{18,... | collective-permute-start | bytes 2359304 | tf_op jit(solution)/shard_map/ppermute | solution.py:110
  282.9 39.4 %collective-permute-start.17 = (bf16[2,2,2,64,768]{4,3,0,2,1:T(8,128)(2,1)S(1)}, bf16[2,2,2,64,768]{4,3,0,2,1:T(8,128)(2,1)S(1)}, u32[]{:S(2)}, u32[]{:S(2)}) collective-permute-start(bf16[2,2,2,64,768]{4,3,0,2,1:T(8,128)(2,1)S(1)} %bitcast.335), channel_id=1, source_target_pairs={{0,4},{2,6},{4,0},{6,2},{8,12},{10,14},{12,8},{14,10},{16,20},{18,... | collective-permute-start | bytes 2359304 | tf_op jit(solution)/shard_map/ppermute | solution.py:110
  285.3 31.8 %collective-permute-start.7 = (bf16[512,1024]{1,0:T(8,128)(2,1)S(1)}, bf16[512,1024]{1,0:T(8,128)(2,1)S(1)}, u32[]{:S(2)}, u32[]{:S(2)}) collective-permute-start(bf16[512,1024]{1,0:T(8,128)(2,1)S(1)} %fusion.48), channel_id=1, source_target_pairs={{0,1},{1,0},{2,3},{3,2},{4,5},{5,4},{6,7},{7,6},{8,9},{9,8},{10,11... | collective-permute-start | bytes 3145736 | tf_op jit(solution)/shard_map/ppermute | solution.py:58
  285.5 6.0 %collective-permute-start.22 = (bf16[2,2,64,256]{3,2,0,1:T(8,128)(2,1)S(1)}, bf16[2,2,64,256]{3,2,0,1:T(8,128)(2,1)S(1)}, u32[]{:S(2)}, u32[]{:S(2)}) collective-permute-start(bf16[2,2,64,256]{3,2,0,1:T(8,128)(2,1)S(1)} %dynamic-slice_bitcast_fusion.23), channel_id=1, source_target_pairs={{0,8},{2,10},{4,12},{6,14},{8,0},{10,2},{12,4},{14,6},{16,24},{18,... | collective-permute-start | bytes 393224 | tf_op jit(solution)/shard_map/ppermute | solution.py:110
  291.4 5.0 %collective-permute-start.26 = (bf16[2,2,64,256]{3,2,0,1:T(8,128)(2,1)S(1)}, bf16[2,2,64,256]{3,2,0,1:T(8,128)(2,1)S(1)}, u32[]{:S(2)}, u32[]{:S(2)}) collective-permute-start(bf16[2,2,64,256]{3,2,0,1:T(8,128)(2,1)S(1)} %dynamic-slice_bitcast_fusion.22), channel_id=1, source_target_pairs={{0,8},{2,10},{4,12},{6,14},{8,0},{10,2},{12,4},{14,6},{16,24},{18,... | collective-permute-start | bytes 393224 | tf_op jit(solution)/shard_map/ppermute | solution.py:110
  292.9 24.3 %copy-start.3 = (bf16[512,1024]{1,0:T(8,128)(2,1)S(1)}, bf16[512,1024]{1,0:T(8,128)(2,1)}, u32[]{:S(2)}) copy-start(bf16[512,1024]{1,0:T(8,128)(2,1)} %param.11) | copy-start | bytes 3145732
  292.9 24.3 %copy-start.24 = (f32[512]{0:T(512)S(1)}, f32[512]{0:T(512)}, u32[]{:S(2)}) copy-start(f32[512]{0:T(512)} %copy-done.23) | copy-start | bytes 6148
  292.9 24.3 %copy-start.26 = (f32[1024]{0:T(1024)S(1)}, f32[1024]{0:T(1024)}, u32[]{:S(2)}) copy-start(f32[1024]{0:T(1024)} %param.13) | copy-start | bytes 12292
  296.4 5.6 %collective-permute-start.23 = (bf16[2,64,256]{2,1,0:T(8,128)(2,1)S(1)}, bf16[2,64,256]{2,1,0:T(8,128)(2,1)S(1)}, u32[]{:S(2)}, u32[]{:S(2)}) collective-permute-start(bf16[2,64,256]{2,1,0:T(8,128)(2,1)S(1)} %dynamic-slice_bitcast_fusion.27), channel_id=1, source_target_pairs={{0,4},{2,6},{4,0},{6,2},{8,12},{10,14},{12,8},{14,10},{16,20},{18,... | collective-permute-start | bytes 196616 | tf_op jit(solution)/shard_map/ppermute | solution.py:110
  302.0 4.3 %collective-permute-start.27 = (bf16[2,64,256]{2,1,0:T(8,128)(2,1)S(1)}, bf16[2,64,256]{2,1,0:T(8,128)(2,1)S(1)}, u32[]{:S(2)}, u32[]{:S(2)}) collective-permute-start(bf16[2,64,256]{2,1,0:T(8,128)(2,1)S(1)} %dynamic-slice_bitcast_fusion.26), channel_id=1, source_target_pairs={{0,2},{2,0},{4,6},{6,4},{8,10},{10,8},{12,14},{14,12},{16,18},{18,... | collective-permute-start | bytes 196616 | tf_op jit(solution)/shard_map/ppermute | solution.py:110
  306.2 5.1 %collective-permute-start.24 = (bf16[64,256]{1,0:T(8,128)(2,1)S(1)}, bf16[64,256]{1,0:T(8,128)(2,1)S(1)}, u32[]{:S(2)}, u32[]{:S(2)}) collective-permute-start(bf16[64,256]{1,0:T(8,128)(2,1)S(1)} %dynamic-slice_bitcast_fusion.29), channel_id=1, source_target_pairs={{0,16},{2,18},{4,20},{6,22},{8,24},{10,26},{12,28},{14,30},{16,0},... | collective-permute-start | bytes 98312 | tf_op jit(solution)/shard_map/ppermute | solution.py:110
  311.4 4.8 %collective-permute-start.28 = (bf16[64,256]{1,0:T(8,128)(2,1)S(1)}, bf16[64,256]{1,0:T(8,128)(2,1)S(1)}, u32[]{:S(2)}, u32[]{:S(2)}) collective-permute-start(bf16[64,256]{1,0:T(8,128)(2,1)S(1)} %dynamic-slice_bitcast_fusion.28), channel_id=1, source_target_pairs={{0,16},{2,18},{4,20},{6,22},{8,24},{10,26},{12,28},{14,30},{16,0},... | collective-permute-start | bytes 98312 | tf_op jit(solution)/shard_map/ppermute | solution.py:110
  316.9 24.2 %slice-start.6 = ((s8[4718592]{0:T(1024)(128)(4,1)}), s8[4194304]{0:T(1024)(128)(4,1)S(1)}, s32[]{:S(2)}) async-start(s8[4718592]{0:T(1024)(128)(4,1)} %bitcast.369), calls=%async_computation.6 | async-start | bytes 8388608
  316.9 24.2 %slice-start.10 = ((s8[4718592]{0:T(1024)(128)(4,1)}), s8[4194304]{0:T(1024)(128)(4,1)S(1)}, s32[]{:S(2)}) async-start(s8[4718592]{0:T(1024)(128)(4,1)} %bitcast.373), calls=%async_computation.10 | async-start | bytes 8388608
  317.1 24.0 %slice-start.7 = ((s8[4718592]{0:T(1024)(128)(4,1)}), s8[524288]{0:T(1024)(128)(4,1)S(1)}, s32[]{:S(2)}) async-start(s8[4718592]{0:T(1024)(128)(4,1)} %bitcast.369), calls=%async_computation.7 | async-start | bytes 1048576
  317.1 24.0 %slice-start.11 = ((s8[4718592]{0:T(1024)(128)(4,1)}), s8[524288]{0:T(1024)(128)(4,1)S(1)}, s32[]{:S(2)}) async-start(s8[4718592]{0:T(1024)(128)(4,1)} %bitcast.373), calls=%async_computation.11 | async-start | bytes 1048576
  319.5 1.2 collective-permute-start.8
  319.5 28.8 %collective-permute-start.14 = (bf16[2,2,64,768]{3,2,0,1:T(8,128)(2,1)S(1)}, bf16[2,2,64,768]{3,2,0,1:T(8,128)(2,1)S(1)}, u32[]{:S(2)}, u32[]{:S(2)}) collective-permute-start(bf16[2,2,64,768]{3,2,0,1:T(8,128)(2,1)S(1)} %dynamic-slice_bitcast_fusion.7), channel_id=1, source_target_pairs={{0,8},{2,10},{4,12},{6,14},{8,0},{10,2},{12,4},{14,6},{16,24},{18,... | collective-permute-start | bytes 1179656 | tf_op jit(solution)/shard_map/ppermute | solution.py:110
  320.8 3.8 %collective-permute-start.9 = (f32[5,512]{1,0:T(8,128)S(1)}, f32[5,512]{1,0:T(8,128)S(1)}, u32[]{:S(2)}, u32[]{:S(2)}) collective-permute-start(f32[5,512]{1,0:T(8,128)S(1)} %pad_maximum_fusion.11), channel_id=1, source_target_pairs={{0,2},{2,0},{4,6},{6,4},{8,10},{10,8},{12,14},{14,12},{16,18},{18,... | collective-permute-start | bytes 30728 | tf_op jit(solution)/shard_map/ppermute | solution.py:129
  324.6 3.8 %collective-permute-start.10 = (f32[5,512]{1,0:T(8,128)S(1)}, f32[5,512]{1,0:T(8,128)S(1)}, u32[]{:S(2)}, u32[]{:S(2)}) collective-permute-start(f32[5,512]{1,0:T(8,128)S(1)} %fusion.92), channel_id=1, source_target_pairs={{0,4},{2,6},{4,0},{6,2},{8,12},{10,14},{12,8},{14,10},{16,20},{18,... | collective-permute-start | bytes 30728 | tf_op jit(solution)/shard_map/ppermute | solution.py:129
  325.9 24.1 %collective-permute-start.18 = (bf16[2,2,64,768]{3,2,0,1:T(8,128)(2,1)S(1)}, bf16[2,2,64,768]{3,2,0,1:T(8,128)(2,1)S(1)}, u32[]{:S(2)}, u32[]{:S(2)}) collective-permute-start(bf16[2,2,64,768]{3,2,0,1:T(8,128)(2,1)S(1)} %dynamic-slice_bitcast_fusion.6), channel_id=1, source_target_pairs={{0,8},{2,10},{4,12},{6,14},{8,0},{10,2},{12,4},{14,6},{16,24},{18,... | collective-permute-start | bytes 1179656 | tf_op jit(solution)/shard_map/ppermute | solution.py:110
  328.4 11.5 %collective-permute-start.11 = (f32[5,512]{1,0:T(8,128)S(1)}, f32[5,512]{1,0:T(8,128)S(1)}, u32[]{:S(2)}, u32[]{:S(2)}) collective-permute-start(f32[5,512]{1,0:T(8,128)S(1)} %add.347), channel_id=1, source_target_pairs={{0,8},{2,10},{4,12},{6,14},{8,0},{10,2},{12,4},{14,6},{16,24},{18,... | collective-permute-start | bytes 30728 | tf_op jit(solution)/shard_map/ppermute | solution.py:129
  339.9 7.2 %collective-permute-start.12 = (f32[5,512]{1,0:T(8,128)S(1)}, f32[5,512]{1,0:T(8,128)S(1)}, u32[]{:S(2)}, u32[]{:S(2)}) collective-permute-start(f32[5,512]{1,0:T(8,128)S(1)} %add.348), channel_id=1, source_target_pairs={{0,16},{2,18},{4,20},{6,22},{8,24},{10,26},{12,28},{14,30},{16,0},... | collective-permute-start | bytes 30728 | tf_op jit(solution)/shard_map/ppermute | solution.py:129
  348.5 6.4 %collective-permute-start.15 = (bf16[2,64,768]{2,1,0:T(8,128)(2,1)S(1)}, bf16[2,64,768]{2,1,0:T(8,128)(2,1)S(1)}, u32[]{:S(2)}, u32[]{:S(2)}) collective-permute-start(bf16[2,64,768]{2,1,0:T(8,128)(2,1)S(1)} %dynamic-slice_bitcast_fusion.15), channel_id=1, source_target_pairs={{0,4},{2,6},{4,0},{6,2},{8,12},{10,14},{12,8},{14,10},{16,20},{18,... | collective-permute-start | bytes 589832 | tf_op jit(solution)/shard_map/ppermute | solution.py:110
  350.2 6.5 %collective-permute-start.19 = (bf16[2,64,768]{2,1,0:T(8,128)(2,1)S(1)}, bf16[2,64,768]{2,1,0:T(8,128)(2,1)S(1)}, u32[]{:S(2)}, u32[]{:S(2)}) collective-permute-start(bf16[2,64,768]{2,1,0:T(8,128)(2,1)S(1)} %dynamic-slice_bitcast_fusion.14), channel_id=1, source_target_pairs={{0,2},{2,0},{4,6},{6,4},{8,10},{10,8},{12,14},{14,12},{16,18},{18,... | collective-permute-start | bytes 589832 | tf_op jit(solution)/shard_map/ppermute | solution.py:110
  354.9 9.5 %collective-permute-start.16 = (bf16[64,768]{1,0:T(8,128)(2,1)S(1)}, bf16[64,768]{1,0:T(8,128)(2,1)S(1)}, u32[]{:S(2)}, u32[]{:S(2)}) collective-permute-start(bf16[64,768]{1,0:T(8,128)(2,1)S(1)} %dynamic-slice_bitcast_fusion.25), channel_id=1, source_target_pairs={{0,16},{2,18},{4,20},{6,22},{8,24},{10,26},{12,28},{14,30},{16,0},... | collective-permute-start | bytes 294920 | tf_op jit(solution)/shard_map/ppermute | solution.py:110
  356.7 8.7 %collective-permute-start.20 = (bf16[64,768]{1,0:T(8,128)(2,1)S(1)}, bf16[64,768]{1,0:T(8,128)(2,1)S(1)}, u32[]{:S(2)}, u32[]{:S(2)}) collective-permute-start(bf16[64,768]{1,0:T(8,128)(2,1)S(1)} %dynamic-slice_bitcast_fusion.24), channel_id=1, source_target_pairs={{0,16},{2,18},{4,20},{6,22},{8,24},{10,26},{12,28},{14,30},{16,0},... | collective-permute-start | bytes 294920 | tf_op jit(solution)/shard_map/ppermute | solution.py:110
  (32 other events, 146.1 us)

commit v2 on v1

--- a/solution.py
+++ b/solution.py
@@ -89,43 +89,69 @@
     return lax.axis_size("dp").bit_length() - 1
 
 
-def dp_orders():
+def exchange(part, step):
     bits = dp_bits()
-    if bits == 4:
-        return ((0, 2, 1, 3), (1, 2, 0, 3))
-    return (tuple(range(bits)), tuple(reversed(range(bits))))
-
-
-def halve(part, order):
+    size, tensors = lax.axis_size("dp"), lax.axis_size("tensor")
+    odd = lax.rem(lax.axis_index("tensor"), 2)
+    me = lax.axis_index("dp")
+    if step > 1:
+        mine = lax.rem(me >> step, 2)
+        sent = lax.dynamic_index_in_dim(part, 1 - mine, bits - 1 - step, keepdims=False)
+        kept = lax.dynamic_index_in_dim(part, mine, bits - 1 - step, keepdims=False)
+        return kept, lax.ppermute(sent, "dp", partners(step))
+    low, high = lax.rem(me, 2), lax.rem(me >> 1, 2)
+    crossed = [
+        ((i * tensors + t), ((i ^ (1 << (step ^ (t % 2)))) * tensors + t))
+        for i in range(size)
+        for t in range(tensors)
+    ]
+    if step == 0:
+        pairs = part.reshape(part.shape[: bits - 2] + (4,) + part.shape[bits:])
+
+        def half(own_low, own_high):
+            blocks = [
+                lax.dynamic_index_in_dim(
+                    pairs, jnp.where(odd == 0, 2 * j + own_low, 2 * own_high + j), bits - 2
+                )
+                for j in range(2)
+            ]
+            return jnp.concatenate(blocks, axis=bits - 2)
+
+        sent, kept = half(1 - low, 1 - high), half(low, high)
+    else:
+        mine = jnp.where(odd == 0, high, low)
+        sent = lax.dynamic_index_in_dim(part, 1 - mine, bits - 2, keepdims=False)
+        kept = lax.dynamic_index_in_dim(part, mine, bits - 2, keepdims=False)
+    return kept, lax.ppermute(sent, ("dp", "tensor"), crossed)
+
+
+def split_rows(part):
     bits = dp_bits()
-    me = lax.axis_index("dp")
-    rows, columns = part.shape
-    part = part.reshape((2,) * bits + (rows >> bits, columns))
-    left = list(reversed(range(bits)))
-    for bit in order:
-        axis = left.index(bit)
-        mine = lax.rem(me >> bit, 2)
-        sent = lax.dynamic_index_in_dim(part, 1 - mine, axis, keepdims=False)
-        kept = lax.dynamic_index_in_dim(part, mine, axis, keepdims=False)
-        received = lax.ppermute(sent, "dp", partners(bit))
-        part = kept.astype(jnp.float32) + received.astype(jnp.float32)
-        left.remove(bit)
-        if left:
-            part = part.astype(jnp.bfloat16)
-    return part
-
-
-def reduce_dp(part):
-    orders = dp_orders()
-    width = part.shape[1] // len(orders)
-    return jnp.concatenate(
-        [halve(part[:, i * width : (i + 1) * width], order) for i, order in enumerate(orders)],
-        axis=1,
-    )
-
-
-def sum_dp(values):
-    for bit in range(dp_bits()):
+    return part.reshape((2,) * bits + (part.shape[0] >> bits, part.shape[1]))
+
+
+def add_half(halves):
+    kept, received = halves
+    return kept.astype(jnp.float32) + received.astype(jnp.float32)
+
+
+def onward(halves, step):
+    return exchange(add_half(halves).astype(jnp.bfloat16), step)
+
+
+def together(values, *halves):
+    values, arrived = lax.optimization_barrier((values, tuple(got for _, got in halves)))
+    return values, *((kept, got) for (kept, _), got in zip(halves, arrived))
+
+
+def finish(halves, step):
+    for later_step in range(step, dp_bits()):
+        halves = onward(halves, later_step)
+    return add_half(halves)
+
+
+def sum_dp(values, first_bit, end_bit):
+    for bit in range(first_bit, end_bit):
         values = values + lax.ppermute(values, "dp", partners(bit))
     return values
 
@@ -194,29 +220,32 @@
     silu_val = gate_val * sigma
     hidden = (silu_val * up_val).astype(jnp.bfloat16)
     cot_rows = cotangent.astype(jnp.float32)
-    down_total = reduce_dp(dot_tn(cot_all, hidden).astype(jnp.bfloat16)).T
-    ffn_out = sum_rows(
-        lambda act: jnp.dot(act, down_weight, preferred_element_type=jnp.float32),
-        own_rows,
-        hidden,
-    )
-    mixed = (middle + ffn_out).astype(jnp.bfloat16)
+    down_part = dot_tn(cot_all, hidden).astype(jnp.bfloat16)
+    cot_all, down_part = lax.optimization_barrier((cot_all, down_part))
     d_hidden = dot_nt(cot_all, down_weight)
     d_gate = (d_hidden * up_val * sigma * (1.0 + gate_val * (1.0 - sigma))).astype(jnp.bfloat16)
     d_up = (d_hidden * silu_val).astype(jnp.bfloat16)
-    gate_total = reduce_dp(dot_tn(norm2_all, d_gate).astype(jnp.bfloat16))
-    up_total = reduce_dp(dot_tn(norm2_all, d_up).astype(jnp.bfloat16))
+    gate_part = dot_tn(norm2_all, d_gate).astype(jnp.bfloat16)
+    up_part = dot_tn(norm2_all, d_up).astype(jnp.bfloat16)
+    down = exchange(split_rows(down_part), 0)
+    gate = exchange(split_rows(gate_part), 0)
+    (d_gate, d_up, up_part), down = together((d_gate, d_up, up_part), down)
+    up = exchange(split_rows(up_part), 0)
+    down = onward(down, 1)
     d_norm2 = sum_rows(
         lambda gate, up: dot_nt(gate, gate_weight) + dot_nt(up, up_weight),
         own_rows,
         d_gate,
         d_up,
     )
+    d_norm2, gate = together(d_norm2, gate)
+    gate = onward(gate, 1)
     d_mid_norm, gain2_part = norm_back(d_norm2, unit2, inv2, norm2_gain)
     d_middle = cot_rows + d_mid_norm
-    d_middle_all = gather_rows(d_middle.astype(jnp.bfloat16))
+    d_middle_low = d_middle.astype(jnp.bfloat16)
+    d_middle_all = gather_rows(d_middle_low)
     d_mixer = dot_nt(d_middle_all, out_weight)
-    out_total = reduce_dp(dot_tn(d_middle_all, mixer_act).astype(jnp.bfloat16)).T
+    out_part = dot_tn(d_middle_all, mixer_act).astype(jnp.bfloat16)
     d_conv = d_mixer * c_gate
     d_c = d_mixer * conv_out
     d_gated = conv_kernel[taps - 1] * d_conv
@@ -230,15 +259,43 @@
     d_projected = jnp.concatenate([d_gated * x_gate, d_c, d_gated * b_gate], axis=1).astype(
         jnp.bfloat16
     )
-    in_total = reduce_dp(dot_tn(norm1_all, d_projected).astype(jnp.bfloat16)).reshape(
-        -1, 3, local_ch
-    )
+    d_projected, down = together(d_projected, down)
+    down = onward(down, 2)
+    in_part = jnp.concatenate(
+        [dot_tn(norm1_all, d_projected).astype(jnp.bfloat16), out_part], axis=1
+    )
+    grad = exchange(split_rows(in_part), 0)
+    (d_projected_all, hidden, in_part), gate, up, down = together(
+        (d_projected, hidden, in_part), gate, up, down
+    )
+    up = onward(up, 1)
+    gate = onward(gate, 2)
+    down = onward(down, 3)
     in_flat = in_weight.reshape(width, -1)
-    d_norm1 = sum_rows(lambda grad: dot_nt(grad, in_flat), own_rows, d_projected)
+    d_norm1 = sum_rows(lambda grad: dot_nt(grad, in_flat), own_rows, d_projected_all)
+    d_norm1, grad, up, gate, down = together(d_norm1, grad, up, gate, down)
+    grad = onward(grad, 1)
+    up = onward(up, 2)
+    gate = onward(gate, 3)
+    down_total = finish(down, 4).T
+    gate_total = finish(gate, 4)
     d_in_norm, gain1_part = norm_back(d_norm1, unit1, inv1, norm1_gain)
     input_grad = d_middle + d_in_norm
     gains = sum_gains(jnp.stack([gain1_part, gain2_part]), local_ch)
-    small = sum_dp(jnp.concatenate([gains, kernel_part], axis=0))
+    small = sum_dp(jnp.concatenate([gains, kernel_part], axis=0), 0, 2)
+    grad = onward(grad, 2)
+    small, grad, up = together(small, grad, up)
+    small = sum_dp(small, 2, dp_bits())
+    up_total = finish(up, 3)
+    in_total = finish(grad, 3)
+    out_total = in_total[:, 3 * local_ch :].T
+    in_total = in_total[:, : 3 * local_ch].reshape(-1, 3, local_ch)
+    ffn_out = sum_rows(
+        lambda act: jnp.dot(act, down_weight, preferred_element_type=jnp.float32),
+        own_rows,
+        hidden,
+    )
+    mixed = (middle + ffn_out).astype(jnp.bfloat16)
     return (
         mixed,
         input_grad,

time: 370 us -> 280 us (0.76)
  waiting for transfers between devices: 134 us -> 76.5 us
  starting transfers between devices: 63.9 us -> 36.5 us
  other arithmetic: 22.6 us -> 31.1 us
  matrix products: 115 us -> 108 us
  local copies, waits for them, and re-layouts: 28.4 us -> 21.9 us
    ppermute x40 -> x16, waiting for transfers between devices: 117 us -> 50.1 us  [the longest x8 28.6 us: exchange(): return (kept, lax.ppermute(sent, 'dp', partners(step)))]
    ppermute x40 -> x16, starting transfers between devices: 57.6 us -> 30.8 us  [the longest x8 18.8 us: exchange(): return (kept, lax.ppermute(sent, 'dp', partners(step)))]
    ppermute x4, waiting for transfers between devices: 14 us -> 22 us  [sum_dp(): values = values + lax.ppermute(values, 'dp', partners(bit))]
    dot_general x1, matrix products: 17.8 us -> 11.8 us  [local(): jnp.dot(norm2_all, gate_weight, preferred_element_type=jnp.float32)]
    convert_element_type x31 -> x13, other arithmetic: 6.07 us -> 11.6 us  [the longest x12 9.71 us: onward(): return exchange(add_half(halves).astype(jnp.bfloat16), step)]
    unnamed x88 -> x64, local copies, waits for them, and re-layouts: 14.1 us -> 9.61 us
    dynamic_slice x20 -> x4, local copies, waits for them, and re-layouts: 5.45 us -> 1.48 us  [half(): lax.dynamic_index_in_dim(pairs, jnp.where(odd == 0, 2 * j + own_low, 2 *...]
  transfers between devices with their start and end apart: 53 -> 29, of which waited for: 24 -> 14; matrix products, arithmetic and copies ran while one was open for 29% -> 39% of each run, Pallas kernels for 0% -> 0%
where the time goes in v2:
time: 280 us; the launch traced here: 276 us
  matrix products  108 us (39%)
  waiting for transfers between devices  76.5 us (27%)
  starting transfers between devices  36.5 us (13%)
  other arithmetic  31.1 us (11%)
  local copies, waits for them, and re-layouts  21.9 us (8%)
    dot_general x8, matrix products, dot_nt(): lax.dot_general(left, right, (((1,), (1,)), ((), ())), preferred_element_...  38.7 us
    dot_general x5, matrix products, dot_tn(): lax.dot_general(left, right, (((0,), (0,)), ((), ())), preferred_element_...  28.9 us
    ppermute x8, waiting for transfers between devices, exchange(): return (kept, lax.ppermute(sent, 'dp', partners(step)))  28.6 us
    ppermute x4, waiting for transfers between devices, sum_dp(): values = values + lax.ppermute(values, 'dp', partners(bit))  22 us
    ppermute x8, waiting for transfers between devices, exchange(): return (kept, lax.ppermute(sent, ('dp', 'tensor'), crossed))  21.5 us
    ppermute x8, starting transfers between devices, exchange(): return (kept, lax.ppermute(sent, 'dp', partners(step)))  18.8 us
    ppermute x8, starting transfers between devices, exchange(): return (kept, lax.ppermute(sent, ('dp', 'tensor'), crossed))  12 us
    dot_general x1, matrix products, local(): jnp.dot(norm2_all, gate_weight, preferred_element_type=jnp.float32)  11.8 us
  transfers between devices with their start and end apart: 29, of which 14 were waited for; matrix products, arithmetic and copies ran while one was open for 39% of the time, Pallas kernels for 0%

profile of v2, /device:TPU:0, one launch (start us, length us, event | category | flops | bytes accessed | tf_op | source)
XLA Modules:
  0.0 276.1 jit_solution(4940230581750011051)
XLA Ops:
  0.7 1.6 fusion.26
  2.3 1.5 fusion.20
  4.8 2.0 collective-permute-done
  6.8 5.6 %fusion.30 = f32[1024,3,512]{2,0,1:T(8,128)S(1)} fusion(bf16[1024,3,512]{2,0,1:T(8,128)(2,1)} %param.14, bf16[512,1024]{1,0:T(8,128)(2,1)} %collective-permute-done, bf16[512,1024]{1,0:T(8,128)(2,1)S(1)} %fusion.20), kind=kOutput, calls=%fused_computation.69 | convolution fusion | flops 3225419776 | bytes 11534336 | tf_op jit(solution)/shard_map/td,dkc->tkc/dot_general | solution.py:192
  12.9 2.1 copy-done.3
  15.1 2.7 multiply_convert_fusion.7
  19.1 2.3 collective-permute-done.1
  22.4 1.3 copy-done.1
  23.7 1.2 multiply_convert_fusion.6
  25.3 4.7 %copy.49 = bf16[1024,3,512]{0,2,1:T(8,128)(2,1)} copy(bf16[1024,3,512]{2,0,1:T(8,128)(2,1)} %param.14) | data formatting | bytes 6291456 | tf_op args[3]
  30.0 1.3 constant_dynamic-update-slice_fusion.1
  31.3 1.4 constant_dynamic-update-slice_fusion
  32.8 11.8 %fusion.75 = f32[1024,2304]{1,0:T(8,128)} fusion(bf16[1024,2304]{1,0:T(8,128)(2,1)} %param.18, bf16[512,1024]{1,0:T(8,128)(2,1)} %collective-permute-done.3, bf16[512,1024]{1,0:T(8,128)(2,1)} %multiply_convert_fusion.6), kind=kOutput, calls=%fused_computation.178 | convolution fusion | flops 4836032512 | bytes 16252928 | tf_op jit(solution)/shard_map/dot_general | solution.py:217
  44.6 11.1 %multiply_convert_fusion.2 = (bf16[1024,2304]{1,0:T(8,128)(2,1)S(1)}, f32[1024,2304]{1,0:T(8,128)}) fusion(f32[1024,2304]{1,0:T(8,128)} %fusion.75, bf16[1024,2304]{1,0:T(8,128)(2,1)S(1)} %bitcast.178, bf16[512,1024]{1,0:T(8,128)(2,1)} %collective-permute-done.3, bf16[512,1024]{1,0:T(8,128)(2,1)} %multiply_convert_fusion.6), kind=kOutput, calls=%fused_computation.2 | convolution fusion | flops 4850188288 | bytes 30408704 | tf_op jit(solution)/shard_map/dot_general | solution.py:218
  55.7 5.9 %convolution_convert_fusion.2 = bf16[1024,2304]{1,0:T(8,128)(2,1)S(1)} fusion(bf16[1024,1024]{1,0:T(8,128)(2,1)S(1)} %constant_dynamic-update-slice_fusion, bf16[1024,2304]{1,0:T(8,128)(2,1)S(1)} %get-tuple-element.43), kind=kOutput, calls=%fused_computation.7 | convolution fusion | flops 4834197504 | bytes 11534336 | tf_op jit(solution)/shard_map/dot_general | solution.py:47
  62.2 1.5 copy.74
  63.8 2.6 collective-permute-start.4
  66.3 14.9 %multiply_convert_fusion = (bf16[1024,2304]{1,0:T(8,128)(2,1)}, bf16[1024,2304]{1,0:T(8,128)(2,1)}) fusion(f32[1024,2304]{1,0:T(8,128)} %fusion.75, f32[1024,2304]{1,0:T(8,128)} %get-tuple-element.107, bf16[1024,1024]{1,0:T(8,128)(2,1)S(1)} %constant_dynamic-update-slice_fusion, bf16[2304,1024]{1,0:T(8,128)(2,1)} %param.20), kind=kOutput, calls=%fused_computation | convolution fusion | flops 4862509056 | bytes 35127296 | tf_op jit(solution)/shard_map/dot_general | solution.py:41
  81.3 8.0 %convolution_convert_fusion = bf16[1024,2304]{1,0:T(8,128)(2,1)S(1)} fusion(bf16[1024,2304]{1,0:T(8,128)(2,1)} %get-tuple-element.35, bf16[512,1024]{1,0:T(8,128)(2,1)} %collective-permute-done.3, bf16[512,1024]{1,0:T(8,128)(2,1)} %multiply_convert_fusion.6), kind=kOutput, calls=%fused_computation.5 | convolution fusion | flops 4838391808 | bytes 11534336 | tf_op jit(solution)/shard_map/dot_general | solution.py:47
  90.2 8.5 %convolution_convert_fusion.1 = bf16[1024,2304]{1,0:T(8,128)(2,1)S(1)} fusion(bf16[1024,2304]{1,0:T(8,128)(2,1)} %get-tuple-element.36, bf16[512,1024]{1,0:T(8,128)(2,1)} %collective-permute-done.3, bf16[512,1024]{1,0:T(8,128)(2,1)} %multiply_convert_fusion.6), kind=kOutput, calls=%fused_computation.6 | convolution fusion | flops 4838391808 | bytes 11534336 | tf_op jit(solution)/shard_map/dot_general | solution.py:47
  98.8 2.6 fusion.12
  101.5 5.7 %add_convert_fusion.5 = bf16[512,1024]{1,0:T(8,128)(2,1)S(1)} fusion(f32[512,1024]{1,0:T(8,128)S(1)} %fusion.12, bf16[1024,2304]{1,0:T(8,128)(2,1)} %param.18, bf16[1024,2304]{1,0:T(8,128)(2,1)} %get-tuple-element.35), kind=kOutput, calls=%fused_computation.83 | convolution fusion | flops 2416967680 | bytes 10223616 | tf_op jit(solution)/shard_map/dot_general | solution.py:41
  107.9 1.1 dynamic-slice_bitcast_fusion.2
  109.1 2.1 collective-permute-start.8
  111.8 1.7 copy.78
  113.5 1.3 collective-permute-start.10
  114.7 4.3 %fusion.16 = f32[512,1024]{1,0:T(8,128)S(1)} fusion(bf16[1024,2304]{1,0:T(8,128)(2,1)S(1)} %bitcast.180, bf16[1024,2304]{1,0:T(8,128)(2,1)} %get-tuple-element.36), kind=kOutput, calls=%fused_computation.42 | convolution fusion | flops 2415919104 | bytes 9175040 | tf_op jit(solution)/shard_map/dot_general | solution.py:41
  119.0 5.6 %convert_add_fusion.6 = f32[512,1024]{1,0:T(8,128)S(1)} fusion(bf16[512,1024]{1,0:T(8,128)(2,1)S(1)} %collective-permute-done.5, f32[512,1024]{1,0:T(8,128)S(1)} %fusion.16, bf16[1024,2304]{1,0:T(8,128)(2,1)} %param.18, bf16[1024,2304]{1,0:T(8,128)(2,1)} %get-tuple-element.35), kind=kOutput, calls=%fused_computation.82 | convolution fusion | flops 2417491968 | bytes 12320768 | tf_op jit(solution)/shard_map/dot_general | solution.py:41
  126.1 1.9 fusion.76
  129.9 1.4 collective-permute-start.9
  131.3 2.0 multiply_reduce_fusion.2
  136.1 2.4 collective-permute-done.8
  138.4 1.6 fusion.7
  140.0 2.3 collective-permute-start.11
  142.3 5.2 %convolution_convert_fusion.3 = bf16[1024,1536]{1,0:T(8,128)(2,1)S(1)} fusion(bf16[1024,1536]{1,0:T(8,128)(2,1)S(1)} %pad_maximum_fusion.1, bf16[512,1024]{1,0:T(8,128)(2,1)} %collective-permute-done, bf16[512,1024]{1,0:T(8,128)(2,1)S(1)} %copy-done.11), kind=kOutput, calls=%fused_computation.13 | convolution fusion | flops 3226992640 | bytes 8388608 | tf_op jit(solution)/shard_map/dot_general | solution.py:47
  147.6 1.3 convolution_convert_fusion.4
  150.2 1.2 collective-permute-start.14
  151.4 12.3 %collective-permute-done.9 = bf16[2,2,64,2304]{3,2,0,1:T(8,128)(2,1)} collective-permute-done((bf16[2,2,64,2304]{3,2,0,1:T(8,128)(2,1)}, bf16[2,2,64,2304]{3,2,0,1:T(8,128)(2,1)}, u32[]{:S(2)}, u32[]{:S(2)}) %collective-permute-start.9) | collective-permute-done | bytes 1179680 | tf_op jit(solution)/shard_map/ppermute | solution.py:125
  163.7 6.0 %collective-permute-done.10 = bf16[2,2,2,64,2304]{4,3,0,1,2:T(8,128)(2,1)} collective-permute-done((bf16[2,2,2,64,2304]{4,3,0,1,2:T(8,128)(2,1)}, bf16[2,2,2,64,2304]{4,3,0,1,2:T(8,128)(2,1)}, u32[]{:S(2)}, u32[]{:S(2)}) %collective-permute-start.10) | collective-permute-done | bytes 2359328 | tf_op jit(solution)/shard_map/ppermute | solution.py:125
  169.7 5.2 %fusion.49 = bf16[512,1024]{1,0:T(8,128)(2,1)} fusion(bf16[2304,1024]{1,0:T(8,128)(2,1)S(1)} %bitcast.182, bf16[1024,2304]{1,0:T(8,128)(2,1)} %copy-done.18), kind=kOutput, calls=%fused_computation.95 | convolution fusion | flops 2416443392 | bytes 8126464 | tf_op jit(solution)/shard_map/dot_general | solution.py:294
  175.0 1.8 fusion.46
  177.3 2.3 add_convert_fusion
  179.8 1.7 collective-permute-start.15
  181.5 1.5 fusion.6
  183.1 1.7 collective-permute-start.16
  184.9 1.2 fusion.55
  186.1 2.7 collective-permute-start.17
  188.8 5.3 %add_convert_fusion.4 = bf16[512,1024]{1,0:T(8,128)(2,1)} fusion(f32[512,1024]{1,0:T(8,128)S(1)} %copy-done.2, bf16[512,1024]{1,0:T(8,128)(2,1)S(1)} %collective-permute-done.12, bf16[2304,1024]{1,0:T(8,128)(2,1)S(1)} %bitcast.184, bf16[1024,2304]{1,0:T(8,128)(2,1)} %copy-done.18), kind=kOutput, calls=%fused_computation.76 | convolution fusion | flops 2418016256 | bytes 11272192 | tf_op jit(solution)/shard_map/dot_general | solution.py:294
  194.1 1.8 convert_add_fusion.5
  195.9 7.7 %collective-permute-done.17 = bf16[64,2304]{1,0:T(8,128)(2,1)S(1)} collective-permute-done((bf16[64,2304]{1,0:T(8,128)(2,1)S(1)}, bf16[64,2304]{1,0:T(8,128)(2,1)S(1)}, u32[]{:S(2)}, u32[]{:S(2)}) %collective-permute-start.17) | collective-permute-done | bytes 294944 | tf_op jit(solution)/shard_map/ppermute | solution.py:101
  205.2 3.6 %fusion.24 = f32[512,1024]{1,0:T(8,128)} fusion(bf16[512,1024]{1,0:T(8,128)(2,1)S(1)} %copy-done.5, f32[512,1024]{1,0:T(8,128)S(1)} %convert_add_fusion.5, f32[512]{0:T(512)S(1)} %broadcast_multiply_fusion.2, f32[1024]{0:T(1024)S(1)} %copy-done.14, f32[512]{0:T(512)S(1)} %copy-done.16, f32[512]{0:T(512)S(1)} %broadcast_multiply_fusion.3, ...), kind=kLoop, calls=%fused_computation.50 | loop fusion | flops 7340032 | bytes 10502144 | tf_op jit(solution)/shard_map/add | solution.py:283
  209.9 1.7 collective-permute-start.21
  212.8 2.5 collective-permute-start.23
  216.3 3.1 %collective-permute-done.19 = f32[5,512]{1,0:T(8,128)S(1)} collective-permute-done((f32[5,512]{1,0:T(8,128)S(1)}, f32[5,512]{1,0:T(8,128)S(1)}, u32[]{:S(2)}, u32[]{:S(2)}) %collective-permute-start.19) | collective-permute-done | bytes 10272 | tf_op jit(solution)/shard_map/ppermute | solution.py:155
  220.1 1.7 collective-permute-start.27
  221.8 3.1 %collective-permute-done.20 = f32[5,512]{1,0:T(8,128)S(1)} collective-permute-done((f32[5,512]{1,0:T(8,128)S(1)}, f32[5,512]{1,0:T(8,128)S(1)}, u32[]{:S(2)}, u32[]{:S(2)}) %collective-permute-start.20) | collective-permute-done | bytes 10272 | tf_op jit(solution)/shard_map/ppermute | solution.py:155
  225.4 2.7 collective-permute-start.22
  228.1 4.2 %collective-permute-done.27 = bf16[64,2304]{1,0:T(8,128)(2,1)S(1)} collective-permute-done((bf16[64,2304]{1,0:T(8,128)(2,1)S(1)}, bf16[64,2304]{1,0:T(8,128)(2,1)S(1)}, u32[]{:S(2)}, u32[]{:S(2)}) %collective-permute-start.27) | collective-permute-done | bytes 294944 | tf_op jit(solution)/shard_map/ppermute | solution.py:101
  233.2 12.5 %collective-permute-done.22 = bf16[2,64,2048]{2,1,0:T(8,128)(2,1)S(1)} collective-permute-done((bf16[2,64,2048]{2,1,0:T(8,128)(2,1)S(1)}, bf16[2,64,2048]{2,1,0:T(8,128)(2,1)S(1)}, u32[]{:S(2)}, u32[]{:S(2)}) %collective-permute-start.22) | collective-permute-done | bytes 524320 | tf_op jit(solution)/shard_map/ppermute | solution.py:101
  246.2 3.7 %collective-permute-start.26 = (bf16[64,2048]{1,0:T(8,128)(2,1)S(1)}, bf16[64,2048]{1,0:T(8,128)(2,1)S(1)}, u32[]{:S(2)}, u32[]{:S(2)}) collective-permute-start(bf16[64,2048]{1,0:T(8,128)(2,1)S(1)} %dynamic-slice_bitcast_fusion.11), channel_id=1, source_target_pairs={{0,16},{2,18},{4,20},{6,22},{8,24},{10,26},{12,28},{14,30},{16,0},... | collective-permute-start | bytes 786440 | tf_op jit(solution)/shard_map/ppermute | solution.py:101
  250.1 1.5 collective-permute-start.25
  251.6 1.6 collective-permute-start.28
  253.1 15.8 %collective-permute-done.25 = f32[5,512]{1,0:T(8,128)S(1)} collective-permute-done((f32[5,512]{1,0:T(8,128)S(1)}, f32[5,512]{1,0:T(8,128)S(1)}, u32[]{:S(2)}, u32[]{:S(2)}) %collective-permute-start.25) | collective-permute-done | bytes 10272 | tf_op jit(solution)/shard_map/ppermute | solution.py:155
  271.7 3.3 %collective-permute-done.28 = bf16[64,2304]{1,0:T(8,128)(2,1)S(1)} collective-permute-done((bf16[64,2304]{1,0:T(8,128)(2,1)S(1)}, bf16[64,2304]{1,0:T(8,128)(2,1)S(1)}, u32[]{:S(2)}, u32[]{:S(2)}) %collective-permute-start.28) | collective-permute-done | bytes 294944 | tf_op jit(solution)/shard_map/ppermute | solution.py:101
  (167 shorter events, 26.3 us)
Async XLA Ops:
  0.6 17.1 %copy-start = (bf16[512,1024]{1,0:T(8,128)(2,1)S(1)}, bf16[512,1024]{1,0:T(8,128)(2,1)}, u32[]{:S(2)}) copy-start(bf16[512,1024]{1,0:T(8,128)(2,1)} %param.16) | copy-start | bytes 3145732
  0.7 3.7 %copy-start.13 = (s32[1,1024]{1,0:T(1,128)S(1)}, s32[1,1024]{1,0:T(1,128)}, u32[]{:S(2)}) copy-start(s32[1,1024]{1,0:T(1,128)} %param.12) | copy-start | bytes 12292
  0.7 4.1 %copy-start.17 = (f32[3,512]{1,0:T(4,128)S(1)}, f32[3,512]{1,0:T(4,128)}, u32[]{:S(2)}) copy-start(f32[3,512]{1,0:T(4,128)} %param.15) | copy-start | bytes 18436
  2.3 4.5 %copy-start.15 = (f32[512]{0:T(512)}, f32[512]{0:T(512)S(1)}, u32[]{:S(2)}) copy-start(f32[512]{0:T(512)S(1)} %add_rsqrt_fusion.1) | copy-start | bytes 6148
  3.8 3.0 %copy-start.10 = (bf16[512,1024]{1,0:T(8,128)(2,1)}, bf16[512,1024]{1,0:T(8,128)(2,1)S(1)}, u32[]{:S(2)}) copy-start(bf16[512,1024]{1,0:T(8,128)(2,1)S(1)} %fusion.20) | copy-start | bytes 3145732
  3.8 2.9 %collective-permute-start = (bf16[512,1024]{1,0:T(8,128)(2,1)S(1)}, bf16[512,1024]{1,0:T(8,128)(2,1)}, u32[]{:S(2)}, u32[]{:S(2)}) collective-permute-start(bf16[512,1024]{1,0:T(8,128)(2,1)S(1)} %fusion.20), channel_id=1, source_target_pairs={{0,1},{1,0},{2,3},{3,2},{4,5},{5,4},{6,7},{7,6},{8,9},{9,8},{10,11... | collective-permute-start | bytes 3145736 | tf_op jit(solution)/shard_map/ppermute | solution.py:58
  12.4 2.7 copy-start.3
  17.8 4.6 %copy-start.8 = (bf16[1024,512]{1,0:T(8,128)(2,1)}, bf16[1024,512]{1,0:T(8,128)(2,1)S(1)}, u32[]{:S(2)}) copy-start(bf16[1024,512]{1,0:T(8,128)(2,1)S(1)} %get-tuple-element.76) | copy-start | bytes 3145732
  17.8 3.6 %copy-start.4 = (bf16[512,1024]{1,0:T(8,128)(2,1)S(1)}, bf16[512,1024]{1,0:T(8,128)(2,1)}, u32[]{:S(2)}) copy-start(bf16[512,1024]{1,0:T(8,128)(2,1)} %param.11) | copy-start | bytes 3145732
  18.5 5.2 %copy-start.12 = (f32[1024]{0:T(1024)S(1)}, f32[1024]{0:T(1024)}, u32[]{:S(2)}) copy-start(f32[1024]{0:T(1024)} %param.17) | copy-start | bytes 12292
  18.5 2.9 %collective-permute-start.1 = (bf16[512,1024]{1,0:T(8,128)(2,1)S(1)}, bf16[512,1024]{1,0:T(8,128)(2,1)S(1)}, u32[]{:S(2)}, u32[]{:S(2)}) collective-permute-start(bf16[512,1024]{1,0:T(8,128)(2,1)S(1)} %convolution_convert_fusion.5), channel_id=1, source_target_pairs={{0,1},{1,0},{2,3},{3,2},{4,5},{5,4},{6,7},{7,6},{8,9},{9,8},{10,11... | collective-permute-start | bytes 3145736 | tf_op jit(solution)/shard_map/ppermute | solution.py:58
  19.0 12.3 %collective-permute-start.2 = (bf16[512,1024]{1,0:T(8,128)(2,1)}, bf16[512,1024]{1,0:T(8,128)(2,1)}, u32[]{:S(2)}, u32[]{:S(2)}) collective-permute-start(bf16[512,1024]{1,0:T(8,128)(2,1)} %param.21), channel_id=1, source_target_pairs={{0,1},{1,0},{2,3},{3,2},{4,5},{5,4},{6,7},{7,6},{8,9},{9,8},{10,11... | collective-permute-start | bytes 3145736 | tf_op jit(solution)/shard_map/ppermute | solution.py:58
  22.4 1.3 copy-start.1
  25.0 7.9 %collective-permute-start.3 = (bf16[512,1024]{1,0:T(8,128)(2,1)}, bf16[512,1024]{1,0:T(8,128)(2,1)}, u32[]{:S(2)}, u32[]{:S(2)}) collective-permute-start(bf16[512,1024]{1,0:T(8,128)(2,1)} %multiply_convert_fusion.6), channel_id=1, source_target_pairs={{0,1},{1,0},{2,3},{3,2},{4,5},{5,4},{6,7},{7,6},{8,9},{9,8},{10,11... | collective-permute-start | bytes 3145736 | tf_op jit(solution)/shard_map/ppermute | solution.py:58
  31.3 13.3 %slice-start.2 = ((s8[4718592]{0:T(1024)(128)(4,1)}), s8[4194304]{0:T(1024)(128)(4,1)S(1)}, s32[]{:S(2)}) async-start(s8[4718592]{0:T(1024)(128)(4,1)} %bitcast.177), calls=%async_computation.2 | async-start | bytes 8388608
  32.8 11.8 %slice-start.3 = ((s8[4718592]{0:T(1024)(128)(4,1)}), s8[524288]{0:T(1024)(128)(4,1)S(1)}, s32[]{:S(2)}) async-start(s8[4718592]{0:T(1024)(128)(4,1)} %bitcast.177), calls=%async_computation.3 | async-start | bytes 1048576
  55.7 5.9 %copy-start.18 = (bf16[1024,2304]{1,0:T(8,128)(2,1)}, bf16[1024,2304]{1,0:T(8,128)(2,1)S(1)}, u32[]{:S(2)}) copy-start(bf16[1024,2304]{1,0:T(8,128)(2,1)S(1)} %get-tuple-element.43) | copy-start | bytes 14155780
  63.8 35.0 %collective-permute-start.4 = (bf16[2,2,2,64,2304]{4,3,0,1,2:T(8,128)(2,1)}, bf16[2,2,2,64,2304]{4,3,0,1,2:T(8,128)(2,1)S(1)}, u32[]{:S(2)}, u32[]{:S(2)}) collective-permute-start(bf16[2,2,2,64,2304]{4,3,0,1,2:T(8,128)(2,1)} %copy.74), channel_id=1, source_target_pairs={{0,2},{1,5},{2,0},{3,7},{4,6},{5,1},{6,4},{7,3},{8,10},{9,13},{10,... | collective-permute-start | bytes 7077896 | tf_op jit(solution)/shard_map/ppermute | solution.py:125
  89.9 8.9 %slice-start.4 = ((s8[4718592]{0:T(1024)(128)(4,1)}), s8[4194304]{0:T(1024)(128)(4,1)S(1)}, s32[]{:S(2)}) async-start(s8[4718592]{0:T(1024)(128)(4,1)} %bitcast.179), calls=%async_computation.4 | async-start | bytes 8388608
  90.0 8.8 %slice-start.10 = ((s8[4718592]{0:T(1024)(128)(4,1)}), s8[524288]{0:T(1024)(128)(4,1)S(1)}, s32[]{:S(2)}) async-start(s8[4718592]{0:T(1024)(128)(4,1)} %bitcast.185), calls=%async_computation.10 | async-start | bytes 1048576
  90.1 35.3 %collective-permute-start.6 = (bf16[2,2,2,64,2304]{4,3,0,1,2:T(8,128)(2,1)S(1)}, bf16[2,2,2,64,2304]{4,3,0,1,2:T(8,128)(2,1)S(1)}, u32[]{:S(2)}, u32[]{:S(2)}) collective-permute-start(bf16[2,2,2,64,2304]{4,3,0,1,2:T(8,128)(2,1)S(1)} %copy.75), channel_id=1, source_target_pairs={{0,2},{1,5},{2,0},{3,7},{4,6},{5,1},{6,4},{7,3},{8,10},{9,13},{10,... | collective-permute-start | bytes 7077896 | tf_op jit(solution)/shard_map/ppermute | solution.py:125
  90.2 8.6 %slice-start.5 = ((s8[4718592]{0:T(1024)(128)(4,1)}), s8[524288]{0:T(1024)(128)(4,1)S(1)}, s32[]{:S(2)}) async-start(s8[4718592]{0:T(1024)(128)(4,1)} %bitcast.179), calls=%async_computation.5 | async-start | bytes 1048576
  90.2 8.6 %slice-start.11 = ((s8[4718592]{0:T(1024)(128)(4,1)}), s8[4194304]{0:T(1024)(128)(4,1)S(1)}, s32[]{:S(2)}) async-start(s8[4718592]{0:T(1024)(128)(4,1)} %bitcast.185), calls=%async_computation.11 | async-start | bytes 8388608
  107.2 11.8 %collective-permute-start.5 = (bf16[512,1024]{1,0:T(8,128)(2,1)S(1)}, bf16[512,1024]{1,0:T(8,128)(2,1)S(1)}, u32[]{:S(2)}, u32[]{:S(2)}) collective-permute-start(bf16[512,1024]{1,0:T(8,128)(2,1)S(1)} %add_convert_fusion.5), channel_id=1, source_target_pairs={{0,1},{1,0},{2,3},{3,2},{4,5},{5,4},{6,7},{7,6},{8,9},{9,8},{10,11... | collective-permute-start | bytes 3145736 | tf_op jit(solution)/shard_map/ppermute | solution.py:58
  109.1 29.3 %collective-permute-start.8 = (bf16[2,2,64,2304]{3,2,0,1:T(8,128)(2,1)}, bf16[2,2,64,2304]{3,2,0,1:T(8,128)(2,1)}, u32[]{:S(2)}, u32[]{:S(2)}) collective-permute-start(bf16[2,2,64,2304]{3,2,0,1:T(8,128)(2,1)} %dynamic-slice_bitcast_fusion.2), channel_id=1, source_target_pairs={{0,4},{1,3},{2,6},{3,1},{4,0},{5,7},{6,2},{7,5},{8,12},{9,11},{10,... | collective-permute-start | bytes 3538952 | tf_op jit(solution)/shard_map/ppermute | solution.py:125
  113.5 56.2 %collective-permute-start.10 = (bf16[2,2,2,64,2304]{4,3,0,1,2:T(8,128)(2,1)}, bf16[2,2,2,64,2304]{4,3,0,1,2:T(8,128)(2,1)}, u32[]{:S(2)}, u32[]{:S(2)}) collective-permute-start(bf16[2,2,2,64,2304]{4,3,0,1,2:T(8,128)(2,1)} %copy.78), channel_id=1, source_target_pairs={{0,2},{1,5},{2,0},{3,7},{4,6},{5,1},{6,4},{7,3},{8,10},{9,13},{10,... | collective-permute-start | bytes 7077896 | tf_op jit(solution)/shard_map/ppermute | solution.py:125
  119.0 6.5 %copy-start.2 = (f32[512,1024]{1,0:T(8,128)S(1)}, f32[512,1024]{1,0:T(8,128)}, u32[]{:S(2)}) copy-start(f32[512,1024]{1,0:T(8,128)} %copy-done.1) | copy-start | bytes 6291460
  126.1 5.2 %slice-start = ((s8[6291456]{0:T(1024)(128)(4,1)}), s8[4194304]{0:T(1024)(128)(4,1)S(1)}, s32[]{:S(2)}) async-start(s8[6291456]{0:T(1024)(128)(4,1)} %bitcast.142), calls=%async_computation | async-start | bytes 8388608
  128.0 3.2 %collective-permute-start.7 = (bf16[512,1024]{1,0:T(8,128)(2,1)S(1)}, bf16[512,1024]{1,0:T(8,128)(2,1)S(1)}, u32[]{:S(2)}, u32[]{:S(2)}) collective-permute-start(bf16[512,1024]{1,0:T(8,128)(2,1)S(1)} %fusion.76), channel_id=1, source_target_pairs={{0,1},{1,0},{2,3},{3,2},{4,5},{5,4},{6,7},{7,6},{8,9},{9,8},{10,11... | collective-permute-start | bytes 3145736 | tf_op jit(solution)/shard_map/ppermute | solution.py:58
  128.1 3.1 %slice-start.1 = ((s8[6291456]{0:T(1024)(128)(4,1)}), s8[2097152]{0:T(1024)(128)(4,1)S(1)}, s32[]{:S(2)}) async-start(s8[6291456]{0:T(1024)(128)(4,1)} %bitcast.142), calls=%async_computation.1 | async-start | bytes 4194304
  128.7 2.5 copy-start.6
  129.9 33.8 %collective-permute-start.9 = (bf16[2,2,64,2304]{3,2,0,1:T(8,128)(2,1)}, bf16[2,2,64,2304]{3,2,0,1:T(8,128)(2,1)}, u32[]{:S(2)}, u32[]{:S(2)}) collective-permute-start(bf16[2,2,64,2304]{3,2,0,1:T(8,128)(2,1)} %dynamic-slice_bitcast_fusion.1), channel_id=1, source_target_pairs={{0,4},{1,3},{2,6},{3,1},{4,0},{5,7},{6,2},{7,5},{8,12},{9,11},{10,... | collective-permute-start | bytes 3538952 | tf_op jit(solution)/shard_map/ppermute | solution.py:125
  136.1 6.3 %copy-start.11 = (bf16[512,1024]{1,0:T(8,128)(2,1)S(1)}, bf16[512,1024]{1,0:T(8,128)(2,1)}, u32[]{:S(2)}) copy-start(bf16[512,1024]{1,0:T(8,128)(2,1)} %copy-done.10) | copy-start | bytes 3145732
  140.0 7.5 %copy-start.9 = (bf16[1024,512]{1,0:T(8,128)(2,1)S(1)}, bf16[1024,512]{1,0:T(8,128)(2,1)}, u32[]{:S(2)}) copy-start(bf16[1024,512]{1,0:T(8,128)(2,1)} %copy-done.8) | copy-start | bytes 3145732
  140.0 29.7 %collective-permute-start.11 = (bf16[2,64,2304]{2,1,0:T(8,128)(2,1)S(1)}, bf16[2,64,2304]{2,1,0:T(8,128)(2,1)}, u32[]{:S(2)}, u32[]{:S(2)}) collective-permute-start(bf16[2,64,2304]{2,1,0:T(8,128)(2,1)S(1)} %dynamic-slice_bitcast_fusion.6), channel_id=1, source_target_pairs={{0,8},{2,10},{4,12},{6,14},{8,0},{10,2},{12,4},{14,6},{16,24},{18,... | collective-permute-start | bytes 1769480 | tf_op jit(solution)/shard_map/ppermute | solution.py:101
  149.5 20.2 %slice-start.6 = ((s8[4718592]{0:T(1024)(128)(4,1)}), s8[4194304]{0:T(1024)(128)(4,1)S(1)}, s32[]{:S(2)}) async-start(s8[4718592]{0:T(1024)(128)(4,1)} %bitcast.181), calls=%async_computation.6 | async-start | bytes 8388608
  149.8 19.9 %slice-start.7 = ((s8[4718592]{0:T(1024)(128)(4,1)}), s8[524288]{0:T(1024)(128)(4,1)S(1)}, s32[]{:S(2)}) async-start(s8[4718592]{0:T(1024)(128)(4,1)} %bitcast.181), calls=%async_computation.7 | async-start | bytes 1048576
  150.2 24.8 %copy-start.7 = (bf16[1024,3,512]{0,2,1:T(8,128)(2,1)S(1)}, bf16[1024,3,512]{0,2,1:T(8,128)(2,1)}, u32[]{:S(2)}) copy-start(bf16[1024,3,512]{0,2,1:T(8,128)(2,1)} %copy.49) | copy-start | bytes 9437188
  150.2 54.3 %collective-permute-start.14 = (bf16[2,2,2,64,2048]{4,3,0,1,2:T(8,128)(2,1)S(1)}, bf16[2,2,2,64,2048]{4,3,0,1,2:T(8,128)(2,1)S(1)}, u32[]{:S(2)}, u32[]{:S(2)}) collective-permute-start(bf16[2,2,2,64,2048]{4,3,0,1,2:T(8,128)(2,1)S(1)} %copy.79), channel_id=1, source_target_pairs={{0,2},{1,5},{2,0},{3,7},{4,6},{5,1},{6,4},{7,3},{8,10},{9,13},{10,... | collective-permute-start | bytes 6291464 | tf_op jit(solution)/shard_map/ppermute | solution.py:125
  175.0 11.2 %collective-permute-start.12 = (bf16[512,1024]{1,0:T(8,128)(2,1)}, bf16[512,1024]{1,0:T(8,128)(2,1)S(1)}, u32[]{:S(2)}, u32[]{:S(2)}) collective-permute-start(bf16[512,1024]{1,0:T(8,128)(2,1)} %fusion.49), channel_id=1, source_target_pairs={{0,1},{1,0},{2,3},{3,2},{4,5},{5,4},{6,7},{7,6},{8,9},{9,8},{10,11... | collective-permute-start | bytes 3145736 | tf_op jit(solution)/shard_map/ppermute | solution.py:58
  176.8 17.3 %collective-permute-start.13 = (bf16[512,1024]{1,0:T(8,128)(2,1)S(1)}, bf16[512,1024]{1,0:T(8,128)(2,1)S(1)}, u32[]{:S(2)}, u32[]{:S(2)}) collective-permute-start(bf16[512,1024]{1,0:T(8,128)(2,1)S(1)} %fusion.46), channel_id=1, source_target_pairs={{0,1},{1,0},{2,3},{3,2},{4,5},{5,4},{6,7},{7,6},{8,9},{9,8},{10,11... | collective-permute-start | bytes 3145736 | tf_op jit(solution)/shard_map/ppermute | solution.py:58
  177.3 11.4 %slice-start.8 = ((s8[4718592]{0:T(1024)(128)(4,1)}), s8[4194304]{0:T(1024)(128)(4,1)S(1)}, s32[]{:S(2)}) async-start(s8[4718592]{0:T(1024)(128)(4,1)} %bitcast.183), calls=%async_computation.8 | async-start | bytes 8388608
  179.7 9.1 %slice-start.9 = ((s8[4718592]{0:T(1024)(128)(4,1)}), s8[524288]{0:T(1024)(128)(4,1)S(1)}, s32[]{:S(2)}) async-start(s8[4718592]{0:T(1024)(128)(4,1)} %bitcast.183), calls=%async_computation.9 | async-start | bytes 1048576
  179.8 24.7 %collective-permute-start.15 = (bf16[2,2,64,2304]{3,2,0,1:T(8,128)(2,1)S(1)}, bf16[2,2,64,2304]{3,2,0,1:T(8,128)(2,1)S(1)}, u32[]{:S(2)}, u32[]{:S(2)}) collective-permute-start(bf16[2,2,64,2304]{3,2,0,1:T(8,128)(2,1)S(1)} %dynamic-slice_bitcast_fusion), channel_id=1, source_target_pairs={{0,4},{1,3},{2,6},{3,1},{4,0},{5,7},{6,2},{7,5},{8,12},{9,11},{10,... | collective-permute-start | bytes 3538952 | tf_op jit(solution)/shard_map/ppermute | solution.py:125
  183.1 21.3 %collective-permute-start.16 = (bf16[2,64,2304]{2,1,0:T(8,128)(2,1)S(1)}, bf16[2,64,2304]{2,1,0:T(8,128)(2,1)S(1)}, u32[]{:S(2)}, u32[]{:S(2)}) collective-permute-start(bf16[2,64,2304]{2,1,0:T(8,128)(2,1)S(1)} %dynamic-slice_bitcast_fusion.5), channel_id=1, source_target_pairs={{0,8},{2,10},{4,12},{6,14},{8,0},{10,2},{12,4},{14,6},{16,24},{18,... | collective-permute-start | bytes 1769480 | tf_op jit(solution)/shard_map/ppermute | solution.py:101
  186.1 17.5 %collective-permute-start.17 = (bf16[64,2304]{1,0:T(8,128)(2,1)S(1)}, bf16[64,2304]{1,0:T(8,128)(2,1)S(1)}, u32[]{:S(2)}, u32[]{:S(2)}) collective-permute-start(bf16[64,2304]{1,0:T(8,128)(2,1)S(1)} %dynamic-slice_bitcast_fusion.10), channel_id=1, source_target_pairs={{0,16},{2,18},{4,20},{6,22},{8,24},{10,26},{12,28},{14,30},{16,0},... | collective-permute-start | bytes 884744 | tf_op jit(solution)/shard_map/ppermute | solution.py:101
  194.0 10.4 %copy-start.5 = (bf16[512,1024]{1,0:T(8,128)(2,1)S(1)}, bf16[512,1024]{1,0:T(8,128)(2,1)}, u32[]{:S(2)}) copy-start(bf16[512,1024]{1,0:T(8,128)(2,1)} %param.11) | copy-start | bytes 3145732
  194.0 10.4 %copy-start.14 = (f32[1024]{0:T(1024)S(1)}, f32[1024]{0:T(1024)}, u32[]{:S(2)}) copy-start(f32[1024]{0:T(1024)} %param.13) | copy-start | bytes 12292
  194.1 10.4 %copy-start.16 = (f32[512]{0:T(512)S(1)}, f32[512]{0:T(512)}, u32[]{:S(2)}) copy-start(f32[512]{0:T(512)} %copy-done.15) | copy-start | bytes 6148
  208.9 6.4 %collective-permute-start.18 = (f32[2,512]{1,0:T(2,128)S(1)}, f32[2,512]{1,0:T(2,128)S(1)}, u32[]{:S(2)}, u32[]{:S(2)}) collective-permute-start(f32[2,512]{1,0:T(2,128)S(1)} %fusion.67), channel_id=1, source_target_pairs={{0,1},{1,0},{2,3},{3,2},{4,5},{5,4},{6,7},{7,6},{8,9},{9,8},{10,11... | collective-permute-start | bytes 12296 | tf_op jit(solution)/shard_map/ppermute | solution.py:58
  209.9 15.0 %collective-permute-start.21 = (bf16[2,2,64,2048]{3,2,0,1:T(8,128)(2,1)S(1)}, bf16[2,2,64,2048]{3,2,0,1:T(8,128)(2,1)S(1)}, u32[]{:S(2)}, u32[]{:S(2)}) collective-permute-start(bf16[2,2,64,2048]{3,2,0,1:T(8,128)(2,1)S(1)} %dynamic-slice_bitcast_fusion.3), channel_id=1, source_target_pairs={{0,4},{1,3},{2,6},{3,1},{4,0},{5,7},{6,2},{7,5},{8,12},{9,11},{10,... | collective-permute-start | bytes 3145736 | tf_op jit(solution)/shard_map/ppermute | solution.py:125
  212.8 20.4 %collective-permute-start.23 = (bf16[2,64,2304]{2,1,0:T(8,128)(2,1)S(1)}, bf16[2,64,2304]{2,1,0:T(8,128)(2,1)S(1)}, u32[]{:S(2)}, u32[]{:S(2)}) collective-permute-start(bf16[2,64,2304]{2,1,0:T(8,128)(2,1)S(1)} %dynamic-slice_bitcast_fusion.4), channel_id=1, source_target_pairs={{0,8},{2,10},{4,12},{6,14},{8,0},{10,2},{12,4},{14,6},{16,24},{18,... | collective-permute-start | bytes 1769480 | tf_op jit(solution)/shard_map/ppermute | solution.py:101
  215.4 4.0 %collective-permute-start.19 = (f32[5,512]{1,0:T(8,128)S(1)}, f32[5,512]{1,0:T(8,128)S(1)}, u32[]{:S(2)}, u32[]{:S(2)}) collective-permute-start(f32[5,512]{1,0:T(8,128)S(1)} %pad_maximum_fusion.17), channel_id=1, source_target_pairs={{0,2},{2,0},{4,6},{6,4},{8,10},{10,8},{12,14},{14,12},{16,18},{18,... | collective-permute-start | bytes 30728 | tf_op jit(solution)/shard_map/ppermute | solution.py:155
  219.4 5.5 %collective-permute-start.20 = (f32[5,512]{1,0:T(8,128)S(1)}, f32[5,512]{1,0:T(8,128)S(1)}, u32[]{:S(2)}, u32[]{:S(2)}) collective-permute-start(f32[5,512]{1,0:T(8,128)S(1)} %fusion.73), channel_id=1, source_target_pairs={{0,4},{2,6},{4,0},{6,2},{8,12},{10,14},{12,8},{14,10},{16,20},{18,... | collective-permute-start | bytes 30728 | tf_op jit(solution)/shard_map/ppermute | solution.py:155
  220.1 12.2 %collective-permute-start.27 = (bf16[64,2304]{1,0:T(8,128)(2,1)S(1)}, bf16[64,2304]{1,0:T(8,128)(2,1)S(1)}, u32[]{:S(2)}, u32[]{:S(2)}) collective-permute-start(bf16[64,2304]{1,0:T(8,128)(2,1)S(1)} %dynamic-slice_bitcast_fusion.9), channel_id=1, source_target_pairs={{0,16},{2,18},{4,20},{6,22},{8,24},{10,26},{12,28},{14,30},{16,0},... | collective-permute-start | bytes 884744 | tf_op jit(solution)/shard_map/ppermute | solution.py:101
  225.4 20.2 %collective-permute-start.22 = (bf16[2,64,2048]{2,1,0:T(8,128)(2,1)S(1)}, bf16[2,64,2048]{2,1,0:T(8,128)(2,1)S(1)}, u32[]{:S(2)}, u32[]{:S(2)}) collective-permute-start(bf16[2,64,2048]{2,1,0:T(8,128)(2,1)S(1)} %dynamic-slice_bitcast_fusion.7), channel_id=1, source_target_pairs={{0,8},{2,10},{4,12},{6,14},{8,0},{10,2},{12,4},{14,6},{16,24},{18,... | collective-permute-start | bytes 1572872 | tf_op jit(solution)/shard_map/ppermute | solution.py:101
  245.6 4.4 %collective-permute-start.24 = (f32[5,512]{1,0:T(8,128)S(1)}, f32[5,512]{1,0:T(8,128)S(1)}, u32[]{:S(2)}, u32[]{:S(2)}) collective-permute-start(f32[5,512]{1,0:T(8,128)S(1)} %add.275), channel_id=1, source_target_pairs={{0,8},{2,10},{4,12},{6,14},{8,0},{10,2},{12,4},{14,6},{16,24},{18,... | collective-permute-start | bytes 30728 | tf_op jit(solution)/shard_map/ppermute | solution.py:155
  246.2 24.0 %collective-permute-start.26 = (bf16[64,2048]{1,0:T(8,128)(2,1)S(1)}, bf16[64,2048]{1,0:T(8,128)(2,1)S(1)}, u32[]{:S(2)}, u32[]{:S(2)}) collective-permute-start(bf16[64,2048]{1,0:T(8,128)(2,1)S(1)} %dynamic-slice_bitcast_fusion.11), channel_id=1, source_target_pairs={{0,16},{2,18},{4,20},{6,22},{8,24},{10,26},{12,28},{14,30},{16,0},... | collective-permute-start | bytes 786440 | tf_op jit(solution)/shard_map/ppermute | solution.py:101
  250.1 18.9 %collective-permute-start.25 = (f32[5,512]{1,0:T(8,128)S(1)}, f32[5,512]{1,0:T(8,128)S(1)}, u32[]{:S(2)}, u32[]{:S(2)}) collective-permute-start(f32[5,512]{1,0:T(8,128)S(1)} %add.279), channel_id=1, source_target_pairs={{0,16},{2,18},{4,20},{6,22},{8,24},{10,26},{12,28},{14,30},{16,0},... | collective-permute-start | bytes 30728 | tf_op jit(solution)/shard_map/ppermute | solution.py:155
  251.6 23.4 %collective-permute-start.28 = (bf16[64,2304]{1,0:T(8,128)(2,1)S(1)}, bf16[64,2304]{1,0:T(8,128)(2,1)S(1)}, u32[]{:S(2)}, u32[]{:S(2)}) collective-permute-start(bf16[64,2304]{1,0:T(8,128)(2,1)S(1)} %dynamic-slice_bitcast_fusion.8), channel_id=1, source_target_pairs={{0,16},{2,18},{4,20},{6,22},{8,24},{10,26},{12,28},{14,30},{16,0},... | collective-permute-start | bytes 884744 | tf_op jit(solution)/shard_map/ppermute | solution.py:101
